TPU v7x, 128 devices: a whole 4x4x4 slice. The times are simulated.
128 devices in a mesh: dp: 8 (over x, core), mp: 16 (over y, z).
Axes of the slice: x: 4, y: 4, z: 4, core: 2. Of those that a mesh axis runs over, the one named last changes fastest.
Arguments:
- tokens: bfloat16 [512, 8192], P('dp', 'mp'), may hold values from -80 to 80
- frozen_gate_weight: bfloat16 [8192, 28672], P('mp', 'dp'), may hold values from -0.198873782 to 0.198873782
- frozen_up_weight: bfloat16 [8192, 28672], P('mp', 'dp'), may hold values from -0.198873782 to 0.198873782
- frozen_down_weight: bfloat16 [28672, 8192], P('dp', 'mp'), may hold values from -0.28347335 to 0.28347335
- gate_left_factor: bfloat16 [8192, 16], P('mp'), may hold values from -0.0625 to 0.0625
- gate_right_factor: bfloat16 [16, 28672], P(None, 'dp'), may hold values from -0.75 to 0.75
- up_left_factor: bfloat16 [8192, 16], P('mp'), may hold values from -0.0625 to 0.0625
- up_right_factor: bfloat16 [16, 28672], P(None, 'dp'), may hold values from -0.75 to 0.75
- down_left_factor: bfloat16 [28672, 16], P('dp'), may hold values from -0.03125 to 0.03125
- down_right_factor: bfloat16 [16, 8192], P(None, 'mp'), may hold values from -0.75 to 0.75
- gate_column_magnitude: float32 [28672], P('dp'), may hold values from 0.5 to 2
- up_column_magnitude: float32 [28672], P('dp'), may hold values from 0.5 to 2
- down_column_magnitude: float32 [8192], P('mp'), may hold values from 0.5 to 2
- cotangent: bfloat16 [512, 8192], P('dp', 'mp'), may hold values from -80 to 80
Outputs:
- feedforward_output: bfloat16 [512, 8192], P('dp', 'mp')
- token_input_gradient: bfloat16 [512, 8192], P('dp', 'mp')
- gate_magnitude_gradient: float32 [28672], P('dp')
- up_magnitude_gradient: float32 [28672], P('dp')
- down_magnitude_gradient: float32 [8192], P('mp')
- gate_right_factor_gradient: float32 [16, 28672], P(None, 'dp')
- gate_left_factor_gradient: float32 [8192, 16], P('mp')
- up_right_factor_gradient: float32 [16, 28672], P(None, 'dp')
- up_left_factor_gradient: float32 [8192, 16], P('mp')
- down_right_factor_gradient: float32 [16, 8192], P(None, 'mp')
- down_left_factor_gradient: float32 [28672, 16], P('dp')
All inputs are finite; a program needn't handle non-finite values.
Results may differ from a plain program's by a relative error of at most 0.03.
Values may be sent and summed in bfloat16 or wider, within the bound.
A program may use at most 192 MiB of HBM per device.

v0:
```python
import jax
import jax.numpy as jnp
from jax import lax
from jax.sharding import Mesh
from jax.sharding import PartitionSpec as P

MP = ("mp_0", "mp_1")


epsilon = 1e-06


def copy_for_each(shard, axis):
    devices = lax.axis_size(axis)
    return lax.all_to_all(
        jnp.broadcast_to(shard[None], (devices, *shard.shape)), axis, 0, 0, tiled=True
    )


def over_copies(shard, axis):
    return copy_for_each(shard, axis).sum(axis=0)


def packed_total(arrays, axis):
    ends = [0]
    for a in arrays:
        ends.append(ends[-1] + a.size)
    subtotal = over_copies(jnp.concatenate([a.ravel() for a in arrays]), axis)
    return tuple((subtotal[b:e].reshape(a.shape) for a, b, e in zip(arrays, ends, ends[1:])))


def joined_along(tiles, dim):
    dims = list(tiles.shape[1:])
    dims[dim] *= tiles.shape[0]
    return jnp.moveaxis(tiles, 0, dim).reshape(dims)


def collect(shard, axis, dim):
    tiles = copy_for_each(shard, axis)
    return joined_along(tiles, dim)


def taken_together(shard, axis):
    everything = copy_for_each(shard, axis)
    return jnp.sum(everything.astype(jnp.float32), axis=0)


def own_rows(terms, axes):
    subtotal = terms.astype(jnp.bfloat16)
    for axis in axes:
        subtotal = lax.psum_scatter(subtotal, axis, scatter_dimension=0, tiled=True)
    return subtotal.astype(jnp.float32)


def cut_along(shard, dim, devices):
    before, after = (shard.shape[:dim], shard.shape[dim + 1 :])
    return jnp.moveaxis(shard.reshape(*before, devices, -1, *after), dim, 0)


def sent_and_summed(shard, axis, dim):
    tiles = cut_along(shard, dim, lax.axis_size(axis))
    arrived = lax.all_to_all(tiles, axis, split_axis=0, concat_axis=0, tiled=True)
    return arrived.astype(jnp.float32).sum(axis=0)


def side_by_side(arrays, axis, dim, along):
    widths = [a.shape[along] for a in arrays]
    both = jnp.concatenate(arrays, axis=along)
    whole = lax.all_gather(both, axis, axis=dim, tiled=True)
    return tuple(jnp.split(whole, [sum(widths[:k]) for k in range(1, len(widths))], axis=along))


def matrix_product(left_side, right_side):
    return jnp.dot(left_side, right_side, preferred_element_type=jnp.float32)


def matrix_product_right_transposed(left_side, right_side):
    return lax.dot_general(
        left_side, right_side, (((1,), (1,)), ((), ())), preferred_element_type=jnp.float32
    )


def matrix_product_left_transposed(left_side, right_side):
    return lax.dot_general(
        left_side, right_side, (((0,), (0,)), ((), ())), preferred_element_type=jnp.float32
    )


def combine_adapter_columns(weight_matrix, left_factor, right_factor):
    combined_weight = weight_matrix.astype(jnp.float32) + matrix_product(left_factor, right_factor)
    return (
        combined_weight.astype(jnp.bfloat16),
        jnp.sum(combined_weight * combined_weight, axis=0),
    )


def activate(pre_pair, scale_gate, scale_up):
    width = scale_gate.shape[0]
    pre_gate = pre_pair[:, :width]
    pre_up = pre_pair[:, width:]
    gate_act = pre_gate * scale_gate
    up_act = pre_up * scale_up
    sigmoid_gate = jax.nn.sigmoid(gate_act)
    silu_gate = gate_act * sigmoid_gate
    hidden_state = (silu_gate * up_act).astype(jnp.bfloat16)
    return (hidden_state, (pre_gate, pre_up, gate_act, up_act, sigmoid_gate, silu_gate))


def gate_backward(grad_hidden, saved, scale_gate, scale_up):
    pre_gate, pre_up, gate_act, up_act, sigmoid_gate, silu_gate = saved
    grad_gate = grad_hidden * up_act * sigmoid_gate * (1.0 + gate_act * (1.0 - sigmoid_gate))
    grad_up = grad_hidden * silu_gate
    gate_logits = (grad_gate * scale_gate).astype(jnp.bfloat16)
    up_logits = (grad_up * scale_up).astype(jnp.bfloat16)
    return (
        gate_logits,
        up_logits,
        jnp.sum(grad_gate * pre_gate, axis=0),
        jnp.sum(grad_up * pre_up, axis=0),
    )


def per_device(
    tokens,
    frozen_gate_weight,
    frozen_up_weight,
    frozen_down_weight,
    gate_left_factor,
    gate_right_factor,
    up_left_factor,
    up_right_factor,
    down_left_factor,
    down_right_factor,
    gate_column_magnitude,
    up_column_magnitude,
    down_column_magnitude,
    cotangent,
):
    combined_gate_weight, gate_squared_columns = combine_adapter_columns(
        frozen_gate_weight, gate_left_factor, gate_right_factor
    )
    combined_up_weight, up_squared_columns = combine_adapter_columns(
        frozen_up_weight, up_left_factor, up_right_factor
    )
    combined_down_weight, down_squared_columns = combine_adapter_columns(
        frozen_down_weight, down_left_factor, down_right_factor
    )
    gate_squared_columns, up_squared_columns = packed_total(
        (gate_squared_columns, up_squared_columns), MP
    )
    down_squared_columns = over_copies(down_squared_columns, "dp")
    gate_column_norm = jnp.sqrt(gate_squared_columns + epsilon)
    up_column_norm = jnp.sqrt(up_squared_columns + epsilon)
    down_column_norm = jnp.sqrt(down_squared_columns + epsilon)
    scale_gate = gate_column_magnitude / gate_column_norm
    scale_up = up_column_magnitude / up_column_norm
    scale_down = down_column_magnitude / down_column_norm
    collected_rows = collect(tokens, "dp", 0)
    local_rows = collected_rows.shape[0] // lax.axis_size(MP)
    row_start = lax.axis_index(MP) * local_rows
    gate_projection_output, up_projection_output = (
        taken_together(
            matrix_product(collected_rows, gate_left_factor).astype(jnp.bfloat16), MP
        ).astype(jnp.float32),
        taken_together(
            matrix_product(collected_rows, up_left_factor).astype(jnp.bfloat16), MP
        ).astype(jnp.float32),
    )
    gate_projection_output = gate_projection_output.astype(jnp.bfloat16)
    up_projection_output = up_projection_output.astype(jnp.bfloat16)
    row_block = collected_rows
    pre_pair = own_rows(
        jnp.concatenate(
            [
                matrix_product(row_block, combined_gate_weight),
                matrix_product(row_block, combined_up_weight),
            ],
            axis=1,
        ),
        MP,
    )
    hidden_local, saved = activate(pre_pair, scale_gate, scale_up)
    hidden_state_full = lax.all_gather(hidden_local, MP, axis=0, tiled=True)
    row_block = hidden_state_full
    down_preactivation = sent_and_summed(
        matrix_product(row_block, combined_down_weight).astype(jnp.bfloat16), "dp", 0
    )
    feedforward_output = (down_preactivation * scale_down).astype(jnp.bfloat16)
    output_cotangent = cotangent.astype(jnp.float32)
    down_logits = (output_cotangent * scale_down).astype(jnp.bfloat16)
    down_projection_output, mag_down_sum = (
        taken_together(
            matrix_product(hidden_state_full, down_left_factor).astype(jnp.bfloat16), "dp"
        ).astype(jnp.float32),
        taken_together(
            jnp.sum(output_cotangent * down_preactivation, axis=0).astype(jnp.bfloat16), "dp"
        ).astype(jnp.float32),
    )
    down_projection_output = down_projection_output.astype(jnp.bfloat16)
    down_magnitude_gradient = mag_down_sum / down_column_norm
    down_logits_full = collect(down_logits, "dp", 0)
    down_backward_rows = (
        taken_together(
            matrix_product_right_transposed(down_logits_full, down_right_factor).astype(
                jnp.bfloat16
            ),
            MP,
        )
        .astype(jnp.float32)
        .astype(jnp.bfloat16)
    )
    down_right_factor_gradient = matrix_product_left_transposed(
        down_projection_output, down_logits_full
    )
    down_left_factor_gradient = matrix_product_left_transposed(
        hidden_state_full, down_backward_rows
    )
    row_block = down_logits_full
    grad_hidden = sent_and_summed(
        matrix_product_right_transposed(row_block, combined_down_weight).astype(jnp.bfloat16), MP, 0
    )
    gate_logits, up_logits, mag_gate_terms, mag_up_terms = gate_backward(
        grad_hidden, saved, scale_gate, scale_up
    )
    proj_gate_rows = lax.dynamic_slice_in_dim(gate_projection_output, row_start, local_rows, 0)
    proj_up_rows = lax.dynamic_slice_in_dim(up_projection_output, row_start, local_rows, 0)
    gate_backward_rows, up_backward_rows = packed_total(
        (
            matrix_product_right_transposed(gate_logits, gate_right_factor),
            matrix_product_right_transposed(up_logits, up_right_factor),
        ),
        "dp",
    )
    gate_backward_rows, up_backward_rows = side_by_side(
        (gate_backward_rows.astype(jnp.bfloat16), up_backward_rows.astype(jnp.bfloat16)), MP, 0, 1
    )
    (
        gate_magnitude_total,
        up_magnitude_total,
        gate_right_factor_gradient,
        up_right_factor_gradient,
    ) = (
        lax.psum(mag_gate_terms.astype(jnp.bfloat16), MP).astype(jnp.float32),
        lax.psum(mag_up_terms.astype(jnp.bfloat16), MP).astype(jnp.float32),
        lax.psum(
            matrix_product_left_transposed(proj_gate_rows, gate_logits).astype(jnp.bfloat16), MP
        ).astype(jnp.float32),
        lax.psum(
            matrix_product_left_transposed(proj_up_rows, up_logits).astype(jnp.bfloat16), MP
        ).astype(jnp.float32),
    )
    z_gate_full, z_up_full = side_by_side((gate_logits, up_logits), MP, 0, 1)
    gate_magnitude_gradient = gate_magnitude_total / gate_column_norm
    up_magnitude_gradient = up_magnitude_total / up_column_norm
    gate_left_factor_gradient = matrix_product_left_transposed(collected_rows, gate_backward_rows)
    up_left_factor_gradient = matrix_product_left_transposed(collected_rows, up_backward_rows)
    token_input_gradient = sent_and_summed(
        (
            matrix_product_right_transposed(z_gate_full, combined_gate_weight)
            + matrix_product_right_transposed(z_up_full, combined_up_weight)
        ).astype(jnp.bfloat16),
        "dp",
        0,
    ).astype(jnp.bfloat16)
    return (
        feedforward_output,
        token_input_gradient,
        gate_magnitude_gradient,
        up_magnitude_gradient,
        down_magnitude_gradient,
        gate_right_factor_gradient,
        gate_left_factor_gradient,
        up_right_factor_gradient,
        up_left_factor_gradient,
        down_right_factor_gradient,
        down_left_factor_gradient,
    )


def solution(mesh):
    torus = Mesh(mesh.devices.reshape(mesh.shape["dp"], 4, 4), ("dp", "mp_0", "mp_1"))
    in_specs = (
        P("dp", MP),
        P(MP, "dp"),
        P(MP, "dp"),
        P("dp", MP),
        P(MP, None),
        P(None, "dp"),
        P(MP, None),
        P(None, "dp"),
        P("dp", None),
        P(None, MP),
        P("dp"),
        P("dp"),
        P(MP),
        P("dp", MP),
    )
    out_specs = (
        P("dp", MP),
        P("dp", MP),
        P("dp"),
        P("dp"),
        P(MP),
        P(None, "dp"),
        P(MP, None),
        P(None, "dp"),
        P(MP, None),
        P(None, MP),
        P("dp", None),
    )
    return jax.shard_map(
        per_device, mesh=torus, in_specs=in_specs, out_specs=out_specs, check_vma=False
    )
```

profile of v0, /device:TPU:1, one launch (start us, length us, event | category | flops | bytes accessed | tf_op | source)
XLA Modules:
  0.0 435.9 jit_solution(9995394842297708845)
XLA Ops:
  7.2 1.7 broadcast_in_dim.20
  8.9 5.8 %all-to-all-start = ((bf16[8,64,512]{2,1,0:T(8,128)(2,1)}), bf16[8,64,512]{2,1,0:T(8,128)(2,1)S(1)}, u32[]{:S(2)}, u32[]{:S(2)}) async-start(bf16[8,64,512]{2,1,0:T(8,128)(2,1)} %broadcast_in_dim.20), calls=%async_computation | async-start | bytes 1048576 | tf_op jit(solution)/shard_map/all_to_all | solution.py:15
  14.8 5.3 %multiply_reduce_fusion.2 = (f32[3584]{0:T(1024)S(1)}, bf16[512,3584]{1,0:T(8,128)(2,1)}) fusion(bf16[512,16]{0,1:T(8,128)(2,1)} %param.18, bf16[16,3584]{1,0:T(8,128)(2,1)} %param.19, bf16[512,3584]{1,0:T(8,128)(2,1)} %param.15), kind=kOutput, calls=%fused_computation.5 | convolution fusion | flops 67891712 | bytes 7485440 | tf_op jit(solution)/shard_map/dot_general | solution.py:74
  20.1 3.2 multiply_reduce_fusion.1
  23.3 0.9 all-to-all-done
  24.2 4.3 fusion
  28.5 3.9 fusion.1
  32.4 5.5 %pad_maximum_fusion = bf16[512,7168]{0,1:T(8,128)(2,1)} fusion(bf16[512,3584]{0,1:T(8,128)(2,1)} %fusion.1, bf16[512,3584]{0,1:T(8,128)(2,1)S(1)} %fusion), kind=kLoop, calls=%fused_computation | loop fusion | flops 14680064 | bytes 14680064 | tf_op jit(solution)/shard_map/concatenate | solution.py:173
  38.0 10.0 %copy.52 = bf16[512,7168]{1,0:T(8,128)(2,1)} copy(bf16[512,7168]{0,1:T(8,128)(2,1)} %pad_maximum_fusion) | data formatting | bytes 14680064
  48.0 0.7 copy-done.6
  48.7 5.2 %multiply_reduce_fusion = (f32[512]{0:T(512)S(1)}, bf16[3584,512]{1,0:T(8,128)(2,1)}) fusion(bf16[3584,16]{0,1:T(8,128)(2,1)S(1)} %copy-done, bf16[16,512]{1,0:T(8,128)(2,1)S(1)} %copy-done.6, bf16[3584,512]{1,0:T(8,128)(2,1)} %param.17), kind=kOutput, calls=%fused_computation.2 | convolution fusion | flops 67894784 | bytes 7473152 | tf_op jit(solution)/shard_map/dot_general | solution.py:74
  53.9 8.4 %all_to_all.69 = f32[8,1,512]{2,1,0:T(1,128)S(1)} all-to-all(f32[8,1,512]{2,1,0:T(1,128)S(1)} %broadcast_in_dim.22), channel_id=1, replica_groups=mesh['dp'=8,'mp_0'=4,'mp_1'=4] {'dp'}, dimensions={0} | all-to-all | bytes 32768 | tf_op jit(solution)/shard_map/all_to_all | solution.py:15
  62.4 0.9 broadcast_in_dim.23
  63.3 4.0 all-to-all-start.4
  67.3 9.5 %all-to-all-done.4 = bf16[8,64,512]{2,1,0:T(8,128)(2,1)S(1)} async-done(((bf16[8,64,512]{2,1,0:T(8,128)(2,1)}), bf16[8,64,512]{2,1,0:T(8,128)(2,1)S(1)}, u32[]{:S(2)}, u32[]{:S(2)}) %all-to-all-start.4) | async-done | bytes 524320 | tf_op jit(solution)/shard_map/all_to_all | solution.py:15
  76.8 1.0 broadcast_in_dim.21
  77.8 7.8 %all-to-all-start.1 = ((f32[16,1,7168]{2,1,0:T(1,128)}), f32[16,1,7168]{2,1,0:T(1,128)S(1)}, u32[]{:S(2)}, u32[]{:S(2)}) async-start(f32[16,1,7168]{2,1,0:T(1,128)} %broadcast_in_dim.21), calls=%async_computation.1 | async-start | bytes 917504 | tf_op jit(solution)/shard_map/all_to_all | solution.py:15
  85.6 6.1 %convolution_convert_fusion = bf16[512,3584]{1,0:T(8,128)(2,1)} fusion(bf16[512,512]{1,0:T(8,128)(2,1)S(1)} %bitcast.57, bf16[3584,512]{1,0:T(8,128)(2,1)} %get-tuple-element.29), kind=kOutput, calls=%fused_computation.8 | convolution fusion | flops 1880883200 | bytes 7864320 | tf_op jit(solution)/shard_map/dot_general | solution.py:78
  91.7 7.4 %all-to-all-done.1 = f32[16,1,7168]{2,1,0:T(1,128)S(1)} async-done(((f32[16,1,7168]{2,1,0:T(1,128)}), f32[16,1,7168]{2,1,0:T(1,128)S(1)}, u32[]{:S(2)}, u32[]{:S(2)}) %all-to-all-start.1) | async-done | bytes 458784 | tf_op jit(solution)/shard_map/all_to_all | solution.py:15
  99.0 6.0 %all-to-all-start.5 = ((bf16[16,32,3584]{2,1,0:T(8,128)(2,1)}), bf16[16,32,3584]{2,1,0:T(8,128)(2,1)}, u32[]{:S(2)}, u32[]{:S(2)}) async-start(bf16[16,32,3584]{2,1,0:T(8,128)(2,1)} %bitcast.60), calls=%async_computation.5 | async-start | bytes 7340032 | tf_op jit(solution)/shard_map/all_to_all | solution.py:62
  105.1 55.5 %reduce-scatter.7.cloned.1.call-done = bf16[128,7168]{1,0:T(8,128)(2,1)} async-done(((bf16[512,7168]{1,0:T(8,128)(2,1)}), bf16[128,7168]{1,0:T(8,128)(2,1)}) %reduce-scatter.7.cloned.1.call-update) | async-done | bytes 1835024
  161.0 6.8 %all-to-all-done.5 = bf16[16,32,3584]{2,1,0:T(8,128)(2,1)} async-done(((bf16[16,32,3584]{2,1,0:T(8,128)(2,1)}), bf16[16,32,3584]{2,1,0:T(8,128)(2,1)}, u32[]{:S(2)}, u32[]{:S(2)}) %all-to-all-start.5) | async-done | bytes 3670048 | tf_op jit(solution)/shard_map/all_to_all | solution.py:62
  167.8 2.6 convert_reduce_fusion
  170.4 24.2 %reduce-scatter.9.cloned.1.call-done = bf16[32,7168]{1,0:T(8,128)(2,1)} async-done(((bf16[128,7168]{1,0:T(8,128)(2,1)}), bf16[32,7168]{1,0:T(8,128)(2,1)}) %reduce-scatter.9.cloned.1.call-update) | async-done | bytes 458768 | tf_op jit(solution)/shard_map/reduce_scatter | solution.py:51
  194.6 1.1 convert_element_type.124
  195.7 1.0 multiply_reduce_fusion.3
  197.0 0.7 broadcast_in_dim.25
  197.8 5.0 %all-to-all-start.8 = ((bf16[16,512,16]{1,2,0:T(8,128)(2,1)}), bf16[16,512,16]{1,2,0:T(8,128)(2,1)S(1)}, u32[]{:S(2)}, u32[]{:S(2)}) async-start(bf16[16,512,16]{1,2,0:T(8,128)(2,1)} %broadcast_in_dim.25), calls=%async_computation.8 | async-start | bytes 524288 | tf_op jit(solution)/shard_map/all_to_all | solution.py:15
  203.0 7.2 %all-to-all-done.8 = bf16[16,512,16]{1,2,0:T(8,128)(2,1)S(1)} async-done(((bf16[16,512,16]{1,2,0:T(8,128)(2,1)}), bf16[16,512,16]{1,2,0:T(8,128)(2,1)S(1)}, u32[]{:S(2)}, u32[]{:S(2)}) %all-to-all-start.8) | async-done | bytes 262176 | tf_op jit(solution)/shard_map/all_to_all | solution.py:15
  210.3 0.7 broadcast_in_dim.27
  211.0 3.5 all-to-all-start.10
  214.6 7.5 %all-to-all-done.10 = bf16[16,512,16]{1,2,0:T(8,128)(2,1)S(1)} async-done(((bf16[16,512,16]{1,2,0:T(8,128)(2,1)}), bf16[16,512,16]{1,2,0:T(8,128)(2,1)S(1)}, u32[]{:S(2)}, u32[]{:S(2)}) %all-to-all-start.10) | async-done | bytes 262176 | tf_op jit(solution)/shard_map/all_to_all | solution.py:15
  222.2 0.9 convolution_convert_fusion.4
  223.1 0.9 convolution_convert_fusion.3
  224.1 0.8 pad_maximum_fusion.1
  225.2 12.9 %all_to_all.70 = bf16[16,512,16]{1,2,0:T(8,128)(2,1)S(1)} all-to-all(bf16[16,512,16]{1,2,0:T(8,128)(2,1)S(1)} %broadcast_in_dim.29), channel_id=1, replica_groups=mesh['dp'=8,'mp_0'=4,'mp_1'=4] {'mp_0','mp_1'}, dimensions={0} | all-to-all | bytes 524288 | tf_op jit(solution)/shard_map/all_to_all | solution.py:15
  238.7 0.6 broadcast_in_dim.26
  239.4 8.5 %all-to-all-start.9 = ((f32[8,1,1024]{2,1,0:T(1,128)}), f32[8,1,1024]{2,1,0:T(1,128)S(1)}, u32[]{:S(2)}, u32[]{:S(2)}) async-start(f32[8,1,1024]{2,1,0:T(1,128)} %broadcast_in_dim.26), calls=%async_computation.9 | async-start | bytes 65536 | tf_op jit(solution)/shard_map/all_to_all | solution.py:15
  247.8 57.0 %all-reduce = (bf16[3584]{0:T(1024)(128)(2,1)S(1)}, bf16[3584]{0:T(1024)(128)(2,1)S(1)}) all-reduce(bf16[3584]{0:T(1024)(128)(2,1)S(1)} %get-tuple-element.12, bf16[3584]{0:T(1024)(128)(2,1)S(1)} %get-tuple-element.11), channel_id=1, replica_groups=mesh['dp'=8,'mp_0'=4,'mp_1'=4] {'mp_0','mp_1'}, use_global_device_ids=true, to_apply=%region_11.0 | all-reduce | flops 7168 | bytes 28672 | tf_op jit(solution)/shard_map/psum | solution.py:243
  304.9 0.6 convert_divide_fusion
  305.8 15.6 %all_gather.11 = bf16[512,32]{1,0:T(8,128)(2,1)S(1)} all-gather(bf16[32,32]{1,0:T(8,128)(2,1)S(1)} %pad_maximum_fusion.3), channel_id=1, replica_groups=mesh['dp'=8,'mp_0'=4,'mp_1'=4] {'mp_0','mp_1'}, dimensions={0}, use_global_device_ids=true | all-gather | bytes 34816 | tf_op jit(solution)/shard_map/all_gather | solution.py:69
  321.4 0.9 convolution_bitcast_fusion
  322.3 3.1 convolution_convert_fusion.5
  325.4 0.7 broadcast_in_dim.28
  326.1 23.8 %all-to-all-start.11 = ((bf16[8,512,16]{1,2,0:T(8,128)(2,1)}), bf16[8,512,16]{1,2,0:T(8,128)(2,1)S(1)}, u32[]{:S(2)}, u32[]{:S(2)}) async-start(bf16[8,512,16]{1,2,0:T(8,128)(2,1)} %broadcast_in_dim.28), calls=%async_computation.11 | async-start | bytes 262144 | tf_op jit(solution)/shard_map/all_to_all | solution.py:15
  349.9 6.0 %fusion.23 = bf16[512,512]{1,0:T(8,128)(2,1)} fusion(bf16[512,3584]{1,0:T(8,128)(2,1)} %all-gather.3.cloned.1.call-done, bf16[3584,512]{1,0:T(8,128)(2,1)} %get-tuple-element.29), kind=kOutput, calls=%fused_computation.28 | convolution fusion | flops 1879310336 | bytes 7864320 | tf_op jit(solution)/shard_map/dot_general | solution.py:74
  355.9 4.8 %all-to-all-start.2 = ((bf16[8,64,512]{2,1,0:T(8,128)(2,1)}), bf16[8,64,512]{2,1,0:T(8,128)(2,1)S(1)}, u32[]{:S(2)}, u32[]{:S(2)}) async-start(bf16[8,64,512]{2,1,0:T(8,128)(2,1)} %bitcast.3), calls=%async_computation.2 | async-start | bytes 1048576 | tf_op jit(solution)/shard_map/all_to_all | solution.py:62
  360.7 0.8 convolution_bitcast_fusion.1
  361.5 1.6 convert_element_type.146
  363.1 1.6 convert_element_type.151
  364.7 3.3 fusion.45
  368.1 2.1 all-to-all-done.2
  370.3 0.7 fusion.28
  371.4 0.7 reduce.9
  372.1 0.6 reshape.111
  372.8 4.1 all-to-all-start.7
  376.9 28.2 %all-gather.5.cloned.1.call-done = bf16[512,7168]{1,0:T(8,128)(2,1)} async-done(((bf16[32,7168]{1,0:T(8,128)(2,1)}), bf16[512,7168]{1,0:T(8,128)(2,1)}) %all-gather.5.cloned.1.call-update) | async-done | bytes 7340048 | tf_op jit(solution)/shard_map/all_gather | solution.py:69
  405.1 5.4 %fusion.2 = f32[512,512]{1,0:T(8,128)S(1)} fusion(bf16[512,7168]{1,0:T(8,128)(2,1)} %all-gather.5.cloned.1.call-done, bf16[512,3584]{1,0:T(8,128)(2,1)} %get-tuple-element.31), kind=kOutput, calls=%fused_computation.15 | convolution fusion | flops 1879048192 | bytes 8388608 | tf_op jit(solution)/shard_map/dot_general | solution.py:78
  410.5 0.9 copy-done.12
  411.4 2.9 fusion.18
  414.2 4.9 %all-to-all-start.6 = ((bf16[8,64,512]{2,1,0:T(8,128)(2,1)}), bf16[8,64,512]{2,1,0:T(8,128)(2,1)S(1)}, u32[]{:S(2)}, u32[]{:S(2)}) async-start(bf16[8,64,512]{2,1,0:T(8,128)(2,1)} %bitcast.6), calls=%async_computation.6 | async-start | bytes 1048576 | tf_op jit(solution)/shard_map/all_to_all | solution.py:62
  419.2 0.8 fusion.44
  420.6 8.1 %all-to-all-done.6 = bf16[8,64,512]{2,1,0:T(8,128)(2,1)S(1)} async-done(((bf16[8,64,512]{2,1,0:T(8,128)(2,1)}), bf16[8,64,512]{2,1,0:T(8,128)(2,1)S(1)}, u32[]{:S(2)}, u32[]{:S(2)}) %all-to-all-start.6) | async-done | bytes 524320 | tf_op jit(solution)/shard_map/all_to_all | solution.py:62
  428.6 0.7 reduce_sum.175
  (73 shorter events, 3.8 us)
Async XLA Ops:
  7.2 40.8 %copy-start = (bf16[3584,16]{0,1:T(8,128)(2,1)S(1)}, bf16[3584,16]{0,1:T(8,128)(2,1)}, u32[]{:S(2)}) copy-start(bf16[3584,16]{0,1:T(8,128)(2,1)} %param.22) | copy-start | bytes 344068
  8.9 15.3 %all-to-all-start = ((bf16[8,64,512]{2,1,0:T(8,128)(2,1)}), bf16[8,64,512]{2,1,0:T(8,128)(2,1)S(1)}, u32[]{:S(2)}, u32[]{:S(2)}) async-start(bf16[8,64,512]{2,1,0:T(8,128)(2,1)} %broadcast_in_dim.20), calls=%async_computation | async-start | bytes 1048576 | tf_op jit(solution)/shard_map/all_to_all | solution.py:15
  14.7 5.4 %copy-start.3 = (bf16[16,3584]{1,0:T(8,128)(2,1)S(1)}, bf16[16,3584]{1,0:T(8,128)(2,1)}, u32[]{:S(2)}) copy-start(bf16[16,3584]{1,0:T(8,128)(2,1)} %param.21) | copy-start | bytes 344068
  14.7 5.4 %copy-start.5 = (bf16[512,16]{0,1:T(8,128)(2,1)S(1)}, bf16[512,16]{0,1:T(8,128)(2,1)}, u32[]{:S(2)}) copy-start(bf16[512,16]{0,1:T(8,128)(2,1)} %param.20) | copy-start | bytes 49156
  14.7 145.9 %reduce-scatter.7.cloned.1.call-start = ((), (), s32[]{:S(2)}) async-start(), calls=%async_computation.17 | async-start | bytes 9175040
  14.7 5.4 %copy-start.11 = (bf16[512,3584]{1,0:T(8,128)(2,1)S(1)}, bf16[512,3584]{1,0:T(8,128)(2,1)}, u32[]{:S(2)}) copy-start(bf16[512,3584]{1,0:T(8,128)(2,1)} %param.16) | copy-start | bytes 11010052
  24.2 4.3 copy-start.13
  47.9 0.7 copy-start.6
  48.7 13.7 %copy-start.9 = (f32[512]{0:T(512)S(1)}, f32[512]{0:T(512)}, u32[]{:S(2)}) copy-start(f32[512]{0:T(512)} %param.26) | copy-start | bytes 6148
  48.7 13.7 %copy-start.1 = (bf16[64,512]{1,0:T(8,128)(2,1)S(1)}, bf16[64,512]{1,0:T(8,128)(2,1)}, u32[]{:S(2)}) copy-start(bf16[64,512]{1,0:T(8,128)(2,1)} %param.27) | copy-start | bytes 196612
  63.3 13.5 %all-to-all-start.4 = ((bf16[8,64,512]{2,1,0:T(8,128)(2,1)}), bf16[8,64,512]{2,1,0:T(8,128)(2,1)S(1)}, u32[]{:S(2)}, u32[]{:S(2)}) async-start(bf16[8,64,512]{2,1,0:T(8,128)(2,1)} %broadcast_in_dim.23), calls=%async_computation.4 | async-start | bytes 1048576 | tf_op jit(solution)/shard_map/all_to_all | solution.py:15
  77.8 21.2 %all-to-all-start.1 = ((f32[16,1,7168]{2,1,0:T(1,128)}), f32[16,1,7168]{2,1,0:T(1,128)S(1)}, u32[]{:S(2)}, u32[]{:S(2)}) async-start(f32[16,1,7168]{2,1,0:T(1,128)} %broadcast_in_dim.21), calls=%async_computation.1 | async-start | bytes 917504 | tf_op jit(solution)/shard_map/all_to_all | solution.py:15
  99.0 61.9 %copy-start.7 = (f32[3584]{0:T(1024)S(1)}, f32[3584]{0:T(1024)}, u32[]{:S(2)}) copy-start(f32[3584]{0:T(1024)} %param.24) | copy-start | bytes 43012
  99.0 61.9 %copy-start.8 = (f32[3584]{0:T(1024)S(1)}, f32[3584]{0:T(1024)}, u32[]{:S(2)}) copy-start(f32[3584]{0:T(1024)} %param.25) | copy-start | bytes 43012
  99.0 68.8 %all-to-all-start.5 = ((bf16[16,32,3584]{2,1,0:T(8,128)(2,1)}), bf16[16,32,3584]{2,1,0:T(8,128)(2,1)}, u32[]{:S(2)}, u32[]{:S(2)}) async-start(bf16[16,32,3584]{2,1,0:T(8,128)(2,1)} %bitcast.60), calls=%async_computation.5 | async-start | bytes 7340032 | tf_op jit(solution)/shard_map/all_to_all | solution.py:62
  105.0 89.6 %reduce-scatter.9.cloned.1.call-start = ((), (), s32[]{:S(2)}) async-start(), calls=%async_computation.18 | async-start | bytes 2293760 | tf_op jit(solution)/shard_map/reduce_scatter | solution.py:51
  160.6 161.7 %all-gather.3.cloned.1.call-start = ((), (), s32[]{:S(2)}) async-start(), calls=%async_computation.15 | async-start | bytes 3899392 | tf_op jit(solution)/shard_map/all_gather | solution.py:183
  161.0 35.8 %copy-start.4 = (bf16[512,16]{0,1:T(8,128)(2,1)S(1)}, bf16[512,16]{0,1:T(8,128)(2,1)}, u32[]{:S(2)}) copy-start(bf16[512,16]{0,1:T(8,128)(2,1)} %param.18) | copy-start | bytes 49156
  197.0 41.1 %copy-start.2 = (bf16[16,3584]{1,0:T(8,128)(2,1)S(1)}, bf16[16,3584]{1,0:T(8,128)(2,1)}, u32[]{:S(2)}) copy-start(bf16[16,3584]{1,0:T(8,128)(2,1)} %param.19) | copy-start | bytes 344068
  197.8 12.5 %all-to-all-start.8 = ((bf16[16,512,16]{1,2,0:T(8,128)(2,1)}), bf16[16,512,16]{1,2,0:T(8,128)(2,1)S(1)}, u32[]{:S(2)}, u32[]{:S(2)}) async-start(bf16[16,512,16]{1,2,0:T(8,128)(2,1)} %broadcast_in_dim.25), calls=%async_computation.8 | async-start | bytes 524288 | tf_op jit(solution)/shard_map/all_to_all | solution.py:15
  211.0 11.2 %all-to-all-start.10 = ((bf16[16,512,16]{1,2,0:T(8,128)(2,1)}), bf16[16,512,16]{1,2,0:T(8,128)(2,1)S(1)}, u32[]{:S(2)}, u32[]{:S(2)}) async-start(bf16[16,512,16]{1,2,0:T(8,128)(2,1)} %broadcast_in_dim.27), calls=%async_computation.10 | async-start | bytes 524288 | tf_op jit(solution)/shard_map/all_to_all | solution.py:15
  214.5 147.0 %all-reduce.4.cloned.1.call-start = ((), (), s32[]{:S(2)}) async-start(), calls=%async_computation.19 | async-start | bytes 458752 | tf_op jit(solution)/shard_map/psum | solution.py:245
  224.0 181.1 %all-gather.5.cloned.1.call-start = ((), (), s32[]{:S(2)}) async-start(), calls=%async_computation.16 | async-start | bytes 7798784 | tf_op jit(solution)/shard_map/all_gather | solution.py:69
  239.4 66.1 %all-to-all-start.9 = ((f32[8,1,1024]{2,1,0:T(1,128)}), f32[8,1,1024]{2,1,0:T(1,128)S(1)}, u32[]{:S(2)}, u32[]{:S(2)}) async-start(f32[8,1,1024]{2,1,0:T(1,128)} %broadcast_in_dim.26), calls=%async_computation.9 | async-start | bytes 65536 | tf_op jit(solution)/shard_map/all_to_all | solution.py:15
  326.1 29.8 %all-to-all-start.11 = ((bf16[8,512,16]{1,2,0:T(8,128)(2,1)}), bf16[8,512,16]{1,2,0:T(8,128)(2,1)S(1)}, u32[]{:S(2)}, u32[]{:S(2)}) async-start(bf16[8,512,16]{1,2,0:T(8,128)(2,1)} %broadcast_in_dim.28), calls=%async_computation.11 | async-start | bytes 262144 | tf_op jit(solution)/shard_map/all_to_all | solution.py:15
  355.9 14.3 %all-to-all-start.2 = ((bf16[8,64,512]{2,1,0:T(8,128)(2,1)}), bf16[8,64,512]{2,1,0:T(8,128)(2,1)S(1)}, u32[]{:S(2)}, u32[]{:S(2)}) async-start(bf16[8,64,512]{2,1,0:T(8,128)(2,1)} %bitcast.3), calls=%async_computation.2 | async-start | bytes 1048576 | tf_op jit(solution)/shard_map/all_to_all | solution.py:62
  372.8 41.5 %all-to-all-start.7 = ((bf16[8,2,256]{2,1,0:T(2,128)(2,1)}), bf16[8,2,256]{2,1,0:T(2,128)(2,1)S(1)}, u32[]{:S(2)}, u32[]{:S(2)}) async-start(bf16[8,2,256]{2,1,0:T(2,128)(2,1)} %reshape.111), calls=%async_computation.7 | async-start | bytes 16384 | tf_op jit(solution)/shard_map/all_to_all | solution.py:15
  405.1 5.4 %copy-start.10 = (bf16[512,7168]{1,0:T(8,128)(2,1)S(1)}, bf16[512,7168]{1,0:T(8,128)(2,1)}, u32[]{:S(2)}) copy-start(bf16[512,7168]{1,0:T(8,128)(2,1)} %all-gather.5.cloned.1.call-done) | copy-start | bytes 22020100
  405.1 6.3 %copy-start.12 = (bf16[512,3584]{1,0:T(8,128)(2,1)S(1)}, bf16[512,3584]{1,0:T(8,128)(2,1)}, u32[]{:S(2)}) copy-start(bf16[512,3584]{1,0:T(8,128)(2,1)} %get-tuple-element.33) | copy-start | bytes 11010052
  414.2 14.4 %all-to-all-start.6 = ((bf16[8,64,512]{2,1,0:T(8,128)(2,1)}), bf16[8,64,512]{2,1,0:T(8,128)(2,1)S(1)}, u32[]{:S(2)}, u32[]{:S(2)}) async-start(bf16[8,64,512]{2,1,0:T(8,128)(2,1)} %bitcast.6), calls=%async_computation.6 | async-start | bytes 1048576 | tf_op jit(solution)/shard_map/all_to_all | solution.py:62
Sparse Core Ops, SparseCore 0:
  48.1 112.4 reduce-scatter.6
  163.0 31.6 reduce-scatter.8
  197.4 52.6 all-gather.2
  253.9 82.0 all-reduce.3
  338.3 66.7 all-gather.4
where the time goes:
time: 438 us; the launch traced here: 436 us
  waiting for transfers between devices  158 us (36%)
  blocking collectives  93.9 us (21%)
  starting transfers between devices  78.5 us (18%)
  matrix products  54.1 us (12%)
  local copies, waits for them, and re-layouts  19.5 us (4%)
  other arithmetic  18.4 us (4%)
  between operations  14 us (3%)
    all_to_all x8, starting transfers between devices, copy_for_each(): lax.all_to_all(jnp.broadcast_to(shard[None], (devices, *shard.shape)), ax...  62.6 us
    psum x1, blocking collectives, per_device(): lax.psum(mag_gate_terms.astype(jnp.bfloat16), MP).astype(jnp.float32)  57 us
    unnamed x6, waiting for transfers between devices  55.6 us
    all_to_all x8, waiting for transfers between devices, copy_for_each(): lax.all_to_all(jnp.broadcast_to(shard[None], (devices, *shard.shape)), ax...  32.5 us
    dot_general x9, matrix products, matrix_product(): return jnp.dot(left_side, right_side, preferred_element_type=jnp.float32)  31.6 us
    all_gather x1, waiting for transfers between devices, side_by_side(): whole = lax.all_gather(both, axis, axis=dim, tiled=True)  28.2 us
    reduce_scatter x1, waiting for transfers between devices, own_rows(): subtotal = lax.psum_scatter(subtotal, axis, scatter_dimension=0, tiled=True)  24.2 us
    all_to_all x2, blocking collectives, copy_for_each(): lax.all_to_all(jnp.broadcast_to(shard[None], (devices, *shard.shape)), ax...  21.3 us
  transfers between devices with their start and end apart: 16, of which 11 were waited for; matrix products, arithmetic and copies ran while one was open for 14% of the time, Pallas kernels for 0%

commit v1 on v0

v1 whole, which is shorter than its diff:
```python
import jax
import jax.numpy as jnp
from jax import lax
from jax.experimental import pallas as pl
from jax.experimental.pallas import tpu as pltpu
from jax.sharding import PartitionSpec as P

F32 = jnp.float32
BF16 = jnp.bfloat16
MESH = pl.DeviceIdType.MESH
EPS = 1e-06

GROUPS = 7
HALF = 256
STAGES = 9


def nn(a, b):
    return jnp.dot(a, b, preferred_element_type=F32)


def nt(a, b):
    return lax.dot_general(a, b, (((1,), (1,)), ((), ())), preferred_element_type=F32)


def kernel(
    tok, cot, wg_hbm, wu_hbm, wd_hbm, gl, gr, ul, ur, dl, dr, lt, dlt, gmag, umag, dmag,
    out, dx, ggm, gum, gdm, ggr, ggl, gur, gul, gdr, gdl,
    wg, wu, wd, gath, xt, zt, sqd_c, sqd_x, scd, nby, nbz, scl, nrm, pry, prz, pr,
    part, r1h, r1f, q, r2h, r2f, hz, mgy, mgz, oacc, xacc, bk,
    fs, fr, th, tf, smc, smx, mdc, mdx,
    wsem, ssem, rsem, ms, mr,
):
    dp = lax.axis_index("dp")
    mp = lax.axis_index("mp")
    x, c = dp // 2, dp % 2
    y, z = mp // 4, mp % 4

    def at_x(i):
        return (i * 2 + c, mp)

    def at_y(i):
        return (dp, i * 4 + z)

    def at_z(i):
        return (dp, y * 4 + i)

    other = (x * 2 + 1 - c, mp)

    def rcopy(src, dst, s, r, dev):
        return pltpu.make_async_remote_copy(
            src_ref=src, dst_ref=dst, send_sem=s, recv_sem=r, device_id=dev, device_id_type=MESH
        )

    def mcopy(src, dst, k, dev):
        return rcopy(src, dst, ms.at[k], mr.at[k], dev)

    def spread(slots, me, place, k):
        return [
            mcopy(slots.at[me], slots.at[me], k + d - 1, place((me + d) % 4)) for d in (1, 2, 3)
        ]

    def start(copies):
        for cp in copies:
            cp.start()

    def wait(copies):
        for cp in copies:
            cp.wait()

    def load_d(j, h):
        return pltpu.make_async_copy(
            wd_hbm.at[pl.ds(pl.multiple_of((j * 2 + h) * HALF, HALF), HALF)],
            wd.at[j, h],
            wsem.at[0, j, h],
        )

    def load_gu(w_hbm, w, k, j, h):
        return pltpu.make_async_copy(
            w_hbm.at[:, pl.ds(pl.multiple_of((j * 2 + h) * HALF, HALF), HALF)],
            w.at[j, h],
            wsem.at[k, j, h],
        )

    @pl.loop(0, GROUPS)
    def _(j):
        for h in (0, 1):
            load_d(j, h).start()

    @pl.loop(0, GROUPS)
    def _(j):
        for h in (0, 1):
            load_gu(wg_hbm, wg, 1, j, h).start()
            load_gu(wu_hbm, wu, 2, j, h).start()

    gath[x, c, 0] = tok[...]
    gath[x, c, 1] = cot[...]

    barrier = pltpu.get_barrier_semaphore()
    for d in (1, 2, 3):
        for dev in (at_x((x + d) % 4), at_y((y + d) % 4), at_z((z + d) % 4)):
            pl.semaphore_signal(barrier, inc=1, device_id=dev, device_id_type=MESH)
    pl.semaphore_signal(barrier, inc=1, device_id=other, device_id_type=MESH)
    pl.semaphore_wait(barrier, 10)

    xr, xl, xo = (x + 1) % 4, (x + 3) % 4, (x + 2) % 4
    own = gath.at[x, c]
    g_own = [
        mcopy(own, own, 0, at_x(xr)),
        mcopy(own, own, 1, at_x(xl)),
        mcopy(own, own, 2, other),
    ]
    start(g_own)

    def merge_down(j, total):
        for h in (0, 1):
            load_d(j, h).wait()
            rows = pl.ds(pl.multiple_of((j * 2 + h) * HALF, HALF), HALF)
            m = wd[j, h].astype(F32) + nn(dl[rows, :], dr[...])
            wd[j, h] = m.astype(BF16)
            total = total + jnp.sum(m * m, axis=0, keepdims=True)
        return total

    sqd_c[c] = lax.fori_loop(0, GROUPS, merge_down, jnp.zeros((1, 512), F32))
    s_core = mcopy(sqd_c.at[c], sqd_c.at[c], 3, other)
    s_core.start()

    wait(g_own[:2])
    lo, ro = gath.at[xl, c], gath.at[xr, c]
    g_fwd = [
        mcopy(gath.at[xl, c, 0], gath.at[xl, c, 0], 4, at_x(xr)),
        mcopy(gath.at[xr, c, 1], gath.at[xr, c, 1], 5, at_x(xl)),
        mcopy(lo, lo, 6, other),
        mcopy(ro, ro, 7, other),
    ]
    start(g_fwd)

    def merge_gu(k, w_hbm, w, left, right, j):
        for h in (0, 1):
            load_gu(w_hbm, w, k, j, h).wait()
            cols = pl.ds(pl.multiple_of((j * 2 + h) * HALF, HALF), HALF)
            m = w[j, h].astype(F32) + nn(left[...], right[:, cols])
            w[j, h] = m.astype(BF16)
            nby[y, k - 1 : k, cols] = jnp.sum(m * m, axis=0, keepdims=True)

    @pl.loop(0, GROUPS)
    def _(j):
        merge_gu(1, wg_hbm, wg, gl, gr, j)

    s_core.wait()
    sqd_x[x] = sqd_c[0] + sqd_c[1]
    s_x = spread(sqd_x, x, at_x, 8)
    start(s_x)
    wait(g_fwd[:2])
    oo = gath.at[xo, c]
    g_last = mcopy(oo, oo, 11, other)
    g_last.start()

    @pl.loop(0, GROUPS)
    def _(j):
        merge_gu(2, wu_hbm, wu, ul, ur, j)

    n_y = spread(nby, y, at_y, 12)
    start(n_y)

    wait(s_x)
    sqd = sqd_x[0] + sqd_x[1] + sqd_x[2] + sqd_x[3]
    normd = jnp.sqrt(sqd + EPS)
    scd[0:1] = normd
    scd[1:2] = dmag[...] / normd
    g_own[2].wait()
    wait(g_fwd[2:])
    g_last.wait()

    for b in range(16):
        px, pc, rows = b // 4, (b // 2) % 2, slice((b % 2) * 32, (b % 2) * 32 + 32)
        p = (b % 4) * 4 + b // 4
        t = gath[px, pc, 0, rows]
        v = (gath[px, pc, 1, rows].astype(F32) * scd[1:2]).astype(BF16)
        xt[0, b * 32 : b * 32 + 32] = t
        xt[1, p * 32 : p * 32 + 32] = t
        zt[0, b * 32 : b * 32 + 32] = v
        zt[1, p * 32 : p * 32 + 32] = v

    pry[y, 0:32] = nt(lt[...], xt[0]).astype(BF16)
    pry[y, 32:48] = nt(dr[...], zt[0]).astype(BF16)
    p_y = spread(pry, y, at_y, 18)
    start(p_y)
    n_z = spread(nbz, z, at_z, 15)
    p_z = spread(prz, z, at_z, 21)
    m_y = spread(mgy, y, at_y, 24)
    m_z = spread(mgz, z, at_z, 27)

    ri = lax.broadcasted_iota(jnp.int32, (512, 512), 0)
    ci = lax.broadcasted_iota(jnp.int32, (512, 512), 1)
    swapped = ((ri // 32) % 4) * 128 + (ri // 128) * 32 + ri % 32
    swap = (swapped == ci).astype(BF16)

    oacc[...] = jnp.zeros_like(oacc)
    xacc[...] = jnp.zeros_like(xacc)
    bk[...] = jnp.zeros_like(bk)

    def geometry(h):
        ia = y + h * (z - y)
        ib = z + h * (y - z)

        def at_a(i):
            return (dp, (i + h * (y - i)) * 4 + z + h * (i - z))

        def at_b(i):
            return (dp, (y + h * (i - y)) * 4 + i + h * (z - i))

        return ia, ib, at_a, at_b

    def copies(s, j, h):
        ia, ib, at_a, at_b = geometry(h)
        ar, al, ao = (ia + 1) % 4, (ia + 3) % 4, (ia + 2) % 4
        br, bl, bo = (ib + 1) % 4, (ib + 3) % 4, (ib + 2) % 4
        if s == 0:
            a = part.at[j, h, :, ao, 0:2], r1h.at[j, h, 0]
            b = part.at[j, h, :, ao, 2:4], r1h.at[j, h, 1]
        elif s == 1:
            a = part.at[j, h, :, ar], r1f.at[j, h, 0]
            b = part.at[j, h, :, al], r1f.at[j, h, 1]
        elif s == 2:
            a = q.at[j, h, :, bo, 0:16], r2h.at[j, h, 0]
            b = q.at[j, h, :, bo, 16:32], r2h.at[j, h, 1]
        elif s == 3:
            a = q.at[j, h, :, br], r2f.at[j, h, 0]
            b = q.at[j, h, :, bl], r2f.at[j, h, 1]
        elif s == 4:
            a = b = (hz.at[j, h, :, ia, ib],) * 2
        elif s == 5:
            a = (hz.at[j, h, :, ia, bl, 0:16],) * 2
            b = (hz.at[j, h, :, ia, br, 16:32],) * 2
        elif s == 6:
            a = b = (hz.at[j, h, :, ia],) * 2
        else:
            a = (hz.at[j, h, :, al, 0:2],) * 2
            b = (hz.at[j, h, :, ar, 2:4],) * 2
        if s in (0, 1, 6, 7):
            dr_, dl_ = at_a(ar), at_a(al)
        else:
            dr_, dl_ = at_b(br), at_b(bl)
        return [
            rcopy(*a, ssem.at[s, j, h, 0], rsem.at[s, j, h, 0], dr_),
            rcopy(*b, ssem.at[s, j, h, 1], rsem.at[s, j, h, 1], dl_),
        ]

    def add_into(ref, extra):
        ref[...] = (ref[...].astype(F32) + extra[...].astype(F32)).astype(BF16)

    def stage(s, j, h):
        ia, ib, _, _ = geometry(h)
        ar, al = (ia + 1) % 4, (ia + 3) % 4
        br, bl = (ib + 1) % 4, (ib + 3) % 4
        cols = pl.ds(pl.multiple_of((j * 2 + h) * HALF, HALF), HALF)
        if s > 0:
            wait(copies(s - 1, j, h))
        if s == 0:
            part[j, h, 0] = nn(xt[h], wg[j, h]).astype(BF16).reshape(4, 4, 32, HALF)
            part[j, h, 1] = nn(xt[h], wu[j, h]).astype(BF16).reshape(4, 4, 32, HALF)
            part[j, h, 2] = nt(zt[h], wd[j, h]).astype(BF16).reshape(4, 4, 32, HALF)
        elif s == 1:
            add_into(part.at[j, h, :, ar, 0:2], r1h.at[j, h, 0])
            add_into(part.at[j, h, :, al, 2:4], r1h.at[j, h, 1])
        elif s == 2:
            q[j, h] = (
                part[j, h, :, ia].astype(F32)
                + r1f[j, h, 0].astype(F32)
                + r1f[j, h, 1].astype(F32)
            ).astype(BF16)
        elif s == 3:
            add_into(q.at[j, h, :, br, 0:16], r2h.at[j, h, 0])
            add_into(q.at[j, h, :, bl, 16:32], r2h.at[j, h, 1])
        elif s == 4:
            pg, pu, gh = (
                q[j, h, k, ib].astype(F32) + r2f[j, h, 0, k].astype(F32) + r2f[j, h, 1, k].astype(F32)
                for k in range(3)
            )
            sg, su = scl[0:1, cols], scl[1:2, cols]
            ga, ua = pg * sg, pu * su
            sig = 1.0 / (1.0 + jnp.exp(-ga))
            silu = ga * sig
            dg = gh * ua * sig * (1.0 + ga * (1.0 - sig))
            du = gh * silu
            hz[j, h, 0, ia, ib] = (silu * ua).astype(BF16)
            hz[j, h, 1, ia, ib] = (dg * sg).astype(BF16)
            hz[j, h, 2, ia, ib] = (du * su).astype(BF16)
            mgy[y, 0:1, cols] = jnp.sum(dg * pg, axis=0, keepdims=True)
            mgy[y, 1:2, cols] = jnp.sum(du * pu, axis=0, keepdims=True)
        elif s == 8:
            hid = hz[j, h, 0].reshape(512, HALF)
            zg = hz[j, h, 1].reshape(512, HALF)
            zu = hz[j, h, 2].reshape(512, HALF)
            oacc[h] += nn(hid, wd[j, h])
            xacc[h] += nt(zg, wg[j, h]) + nt(zu, wu[j, h])
            ggr[:, cols] = nn(pr[h, 0:16], zg)
            gur[:, cols] = nn(pr[h, 16:32], zu)
            gdl[:, cols] = nn(pr[h, 32:48], hid)
            bk[h, 0:16] += nt(gr[:, cols], zg)
            bk[h, 16:32] += nt(ur[:, cols], zu)
            bk[h, 32:48] += nt(dlt[:, cols], hid)
        if s < 8:
            start(copies(s, j, h))

    @pl.loop(0, GROUPS + STAGES - 1)
    def _(t):
        @pl.when(t == 4)
        def _():
            wait(n_z)
            for k, mag in enumerate((gmag, umag)):
                n = jnp.sqrt(
                    nbz[0, k : k + 1] + nbz[1, k : k + 1] + nbz[2, k : k + 1] + nbz[3, k : k + 1] + EPS
                )
                nrm[k : k + 1] = n
                scl[k : k + 1] = mag[...] / n

        @pl.when(t == 7)
        def _():
            wait(p_z)
            total = sum(prz[k].astype(F32) for k in range(4)).astype(BF16)
            pr[0] = total
            pr[1] = nn(total, swap).astype(BF16)

        for s in range(STAGES):
            j = t - s

            @pl.when(jnp.logical_and(j >= 0, j < GROUPS))
            def _():
                @pl.loop(0, 2)
                def _(h):
                    stage(s, j, h)

        @pl.when(t == 0)
        def _():
            wait(n_y)
            nbz[z] = nby[0] + nby[1] + nby[2] + nby[3]
            start(n_z)

        @pl.when(t == 1)
        def _():
            wait(p_y)
            prz[z] = sum(pry[k].astype(F32) for k in range(4)).astype(BF16)
            start(p_z)

        @pl.when(t == GROUPS + 3)
        def _():
            start(m_y)

        @pl.when(t == GROUPS + 5)
        def _():
            wait(m_y)
            mgz[z] = mgy[0] + mgy[1] + mgy[2] + mgy[3]
            start(m_z)

    md = jnp.zeros((1, 512), F32)
    for b in range(16):
        px, pc, rows = b // 4, (b // 2) % 2, slice((b % 2) * 32, (b % 2) * 32 + 32)
        p = (b % 4) * 4 + b // 4
        o = oacc[0, b * 32 : b * 32 + 32] + oacc[1, p * 32 : p * 32 + 32]
        v = xacc[0, b * 32 : b * 32 + 32] + xacc[1, p * 32 : p * 32 + 32]
        md = md + jnp.sum(o * gath[px, pc, 1, rows].astype(F32), axis=0, keepdims=True)
        fs[pc, 0, px, rows] = o.astype(BF16)
        fs[pc, 1, px, rows] = v.astype(BF16)
    f_core = mcopy(fs.at[1 - c], fr, 30, other)
    f_core.start()
    mdc[c] = md
    smc[c] = (bk[0] + nn(bk[1].astype(BF16), swap)).astype(BF16)
    md_core = mcopy(mdc.at[c], mdc.at[c], 31, other)
    sm_core = mcopy(smc.at[c], smc.at[c], 32, other)
    start([md_core, sm_core])
    f_core.wait()
    add_into(fs.at[c], fr)
    f_half = [
        mcopy(fs.at[c, :, xo, 0:32], th.at[0], 33, at_x(xr)),
        mcopy(fs.at[c, :, xo, 32:64], th.at[1], 34, at_x(xl)),
    ]
    start(f_half)
    wait([md_core, sm_core])
    mdx[x] = mdc[0] + mdc[1]
    smx[x] = (smc[0].astype(F32) + smc[1].astype(F32)).astype(BF16)
    sm_x = spread(smx, x, at_x, 37)
    md_x = spread(mdx, x, at_x, 40)
    start(sm_x)
    start(md_x)
    wait(f_half)
    add_into(fs.at[c, :, xr, 0:32], th.at[0])
    add_into(fs.at[c, :, xl, 32:64], th.at[1])
    f_full = [
        mcopy(fs.at[c, :, xr], tf.at[0], 35, at_x(xr)),
        mcopy(fs.at[c, :, xl], tf.at[1], 36, at_x(xl)),
    ]
    start(f_full)

    wait(m_z)
    mags = (mgz[0] + mgz[1] + mgz[2] + mgz[3]) / nrm[...]
    ggm[...] = mags[0:1]
    gum[...] = mags[1:2]
    wait(sm_x)
    back = sum(smx[k].astype(F32) for k in range(4)).astype(BF16)
    lg = nn(back[0:32], xt[0])
    ggl[...] = lg[0:16]
    gul[...] = lg[16:32]
    gdr[...] = nn(back[32:48], zt[0])
    wait(md_x)
    gdm[...] = (mdx[0] + mdx[1] + mdx[2] + mdx[3]) / scd[0:1]
    wait(f_full)
    tot = fs[c, :, x].astype(F32) + tf[0].astype(F32) + tf[1].astype(F32)
    out[...] = (tot[0] * scd[1:2]).astype(BF16)
    dx[...] = tot[1].astype(BF16)


def per_device(tok, fg, fu, fd, gl, gr, ul, ur, dl, dr, gmag, umag, dmag, cot):
    vm = pl.BlockSpec(memory_space=pltpu.VMEM)
    hbm = pl.BlockSpec(memory_space=pl.ANY)
    f = jax.ShapeDtypeStruct
    V = pltpu.VMEM
    G, C = GROUPS, HALF
    lt = jnp.concatenate([gl.T, ul.T], axis=0)
    call = pl.pallas_call(
        kernel,
        out_shape=(
            f((64, 512), BF16), f((64, 512), BF16),
            f((1, 3584), F32), f((1, 3584), F32), f((1, 512), F32),
            f((16, 3584), F32), f((16, 512), F32), f((16, 3584), F32), f((16, 512), F32),
            f((16, 512), F32), f((16, 3584), F32),
        ),
        in_specs=[vm, vm, hbm, hbm, hbm] + [vm] * 11,
        out_specs=(vm,) * 11,
        scratch_shapes=[
            V((G, 2, 512, C), BF16), V((G, 2, 512, C), BF16), V((G, 2, C, 512), BF16),
            V((4, 2, 2, 64, 512), BF16), V((2, 512, 512), BF16), V((2, 512, 512), BF16),
            V((2, 1, 512), F32), V((4, 1, 512), F32), V((2, 512), F32),
            V((4, 2, 3584), F32), V((4, 2, 3584), F32), V((2, 3584), F32), V((2, 3584), F32),
            V((4, 48, 512), BF16), V((4, 48, 512), BF16), V((2, 48, 512), BF16),
            V((G, 2, 3, 4, 4, 32, C), BF16),
            V((G, 2, 2, 3, 2, 32, C), BF16), V((G, 2, 2, 3, 4, 32, C), BF16),
            V((G, 2, 3, 4, 32, C), BF16),
            V((G, 2, 2, 3, 16, C), BF16), V((G, 2, 2, 3, 32, C), BF16),
            V((G, 2, 3, 4, 4, 32, C), BF16),
            V((4, 2, 3584), F32), V((4, 2, 3584), F32),
            V((2, 512, 512), F32), V((2, 512, 512), F32), V((2, 48, 512), F32),
            V((2, 2, 4, 64, 512), BF16), V((2, 4, 64, 512), BF16),
            V((2, 2, 32, 512), BF16), V((2, 2, 64, 512), BF16),
            V((2, 48, 512), BF16), V((4, 48, 512), BF16),
            V((2, 1, 512), F32), V((4, 1, 512), F32),
            pltpu.SemaphoreType.DMA((3, G, 2)),
            pltpu.SemaphoreType.DMA((8, G, 2, 2)),
            pltpu.SemaphoreType.DMA((8, G, 2, 2)),
            pltpu.SemaphoreType.DMA((43,)),
            pltpu.SemaphoreType.DMA((43,)),
        ],
        compiler_params=pltpu.CompilerParams(
            collective_id=0, has_side_effects=True, vmem_limit_bytes=63 * 1024 * 1024
        ),
    )
    o, d, ggm, gum, gdm, ggr, ggl, gur, gul, gdr, gdl = call(
        tok, cot, fg, fu, fd, gl, gr, ul, ur, dl, dr, lt, dl.T,
        gmag.reshape(1, -1), umag.reshape(1, -1), dmag.reshape(1, -1),
    )
    return (
        o, d, ggm.reshape(-1), gum.reshape(-1), gdm.reshape(-1),
        ggr, ggl.T, gur, gul.T, gdr, gdl.T,
    )


def solution(mesh):
    in_specs = (
        P("dp", "mp"), P("mp", "dp"), P("mp", "dp"), P("dp", "mp"),
        P("mp", None), P(None, "dp"), P("mp", None), P(None, "dp"),
        P("dp", None), P(None, "mp"), P("dp"), P("dp"), P("mp"), P("dp", "mp"),
    )
    out_specs = (
        P("dp", "mp"), P("dp", "mp"), P("dp"), P("dp"), P("mp"),
        P(None, "dp"), P("mp", None), P(None, "dp"), P("mp", None), P(None, "mp"), P("dp", None),
    )
    return jax.shard_map(
        per_device, mesh=mesh, in_specs=in_specs, out_specs=out_specs, check_vma=False
    )
```

time: 438 us -> 187 us (0.43)
  Pallas kernels: 0 us -> 159 us
  waiting for transfers between devices: 158 us -> 0 us
  blocking collectives: 93.9 us -> 0 us
  starting transfers between devices: 78.5 us -> 0 us
  matrix products: 54.1 us -> 0 us
  other arithmetic: 18.4 us -> 4.06 us
  between operations: 14 us -> 0.66 us
    pallas_call x0 -> x1, Pallas kernels: none -> 159 us  [per_device(): call(tok, cot, fg, fu, fd, gl, gr, ul, ur, dl, dr, lt, dl.T, gmag.reshape...]
    all_to_all x11 -> x0, starting transfers between devices: 78.3 us -> none  [the longest x8 62.6 us: copy_for_each(): lax.all_to_all(jnp.broadcast_to(shard[None], (devices, *shard.shape)), ax...]
    psum x1 -> x0, blocking collectives: 57 us -> none  [per_device(): lax.psum(mag_gate_terms.astype(jnp.bfloat16), MP).astype(jnp.float32)]
    unnamed x6 -> x0, waiting for transfers between devices: 55.6 us -> none
    dot_general x21 -> x0, matrix products: 54.1 us -> none  [the longest x9 31.6 us: matrix_product(): return jnp.dot(left_side, right_side, preferred_element_type=jnp.float32)]
    all_to_all x11 -> x0, waiting for transfers between devices: 49.5 us -> none  [the longest x8 32.5 us: copy_for_each(): lax.all_to_all(jnp.broadcast_to(shard[None], (devices, *shard.shape)), ax...]
    all_gather x2 -> x0, waiting for transfers between devices: 28.2 us -> none  [the longest x1 28.2 us: side_by_side(): whole = lax.all_gather(both, axis, axis=dim, tiled=True)]
    reduce_scatter x1 -> x0, waiting for transfers between devices: 24.2 us -> none  [own_rows(): subtotal = lax.psum_scatter(subtotal, axis, scatter_dimension=0, tiled=True)]
  transfers between devices with their start and end apart: 16 -> 0, of which waited for: 11 -> 0; matrix products, arithmetic and copies ran while one was open for 14% -> 0% of each run, Pallas kernels for 0% -> 0%
where the time goes in v1:
time: 187 us; the launch traced here: 184 us
  Pallas kernels  159 us (85%)
  local copies, waits for them, and re-layouts  21 us (11%)
  other arithmetic  4.06 us (2%)
    pallas_call x1, Pallas kernels, per_device(): call(tok, cot, fg, fu, fd, gl, gr, ul, ur, dl, dr, lt, dl.T, gmag.reshape...  159 us
    unnamed x12, local copies, waits for them, and re-layouts  18.3 us

profile of v1, /device:TPU:1, one launch (start us, length us, event | category | flops | bytes accessed | tf_op | source)
XLA Modules:
  0.0 184.3 jit_solution(8238514629469416581)
XLA Ops:
  0.6 1.3 reshape.40.gmag
  2.0 1.3 reshape.41.umag
  3.3 1.4 pad_maximum_fusion.lt
  4.6 1.5 copy.25.gl
  6.1 1.5 copy.26.ul
  7.6 2.1 %copy.27.dl = bf16[3584,16]{1,0:T(8,128)(2,1)} copy(bf16[3584,16]{0,1:T(8,128)(2,1)} %param.22) | data formatting | bytes 229376 | tf_op args[8]
  9.7 158.6 %shard_map.221 = (bf16[64,512]{1,0:T(8,128)(2,1)}, bf16[64,512]{1,0:T(8,128)(2,1)}, f32[1,3584]{1,0:T(1,128)}, f32[1,3584]{1,0:T(1,128)}, f32[1,512]{1,0:T(1,128...) custom-call(bf16[64,512]{1,0:T(8,128)(2,1)} %tok.1, ...), custom_call_target="tpu_custom_call" | custom-call | tf_op jit(solution)/shard_map/pallas_call | solution.py:458
  168.4 1.4 reduce
  169.7 1.4 reduce.1
  171.1 1.5 copy.37
  172.6 1.5 copy.38
  174.0 1.3 copy.39
  175.3 1.6 copy.40
  176.9 1.4 copy.41
  178.3 1.6 copy.42
  179.9 1.4 copy.43
  181.3 1.4 copy.44
  182.7 1.6 copy.45

commit v2 on v1

--- a/solution.py
+++ b/solution.py
@@ -23,8 +23,12 @@
     return lax.dot_general(a, b, (((1,), (1,)), ((), ())), preferred_element_type=F32)
 
 
+def tn(a, b):
+    return lax.dot_general(a, b, (((0,), (0,)), ((), ())), preferred_element_type=F32)
+
+
 def kernel(
-    tok, cot, wg_hbm, wu_hbm, wd_hbm, gl, gr, ul, ur, dl, dr, lt, dlt, gmag, umag, dmag,
+    tok, cot, wg_hbm, wu_hbm, wd_hbm, glt, gr, ult, ur, dlt, dr, gmag, umag, dmag,
     out, dx, ggm, gum, gdm, ggr, ggl, gur, gul, gdr, gdl,
     wg, wu, wd, gath, xt, zt, sqd_c, sqd_x, scd, nby, nbz, scl, nrm, pry, prz, pr,
     part, r1h, r1f, q, r2h, r2f, hz, mgy, mgz, oacc, xacc, bk,
@@ -116,7 +120,7 @@
         for h in (0, 1):
             load_d(j, h).wait()
             rows = pl.ds(pl.multiple_of((j * 2 + h) * HALF, HALF), HALF)
-            m = wd[j, h].astype(F32) + nn(dl[rows, :], dr[...])
+            m = wd[j, h].astype(F32) + tn(dlt[:, rows], dr[...])
             wd[j, h] = m.astype(BF16)
             total = total + jnp.sum(m * m, axis=0, keepdims=True)
         return total
@@ -139,13 +143,13 @@
         for h in (0, 1):
             load_gu(w_hbm, w, k, j, h).wait()
             cols = pl.ds(pl.multiple_of((j * 2 + h) * HALF, HALF), HALF)
-            m = w[j, h].astype(F32) + nn(left[...], right[:, cols])
+            m = w[j, h].astype(F32) + tn(left[...], right[:, cols])
             w[j, h] = m.astype(BF16)
             nby[y, k - 1 : k, cols] = jnp.sum(m * m, axis=0, keepdims=True)
 
     @pl.loop(0, GROUPS)
     def _(j):
-        merge_gu(1, wg_hbm, wg, gl, gr, j)
+        merge_gu(1, wg_hbm, wg, glt, gr, j)
 
     s_core.wait()
     sqd_x[x] = sqd_c[0] + sqd_c[1]
@@ -158,7 +162,7 @@
 
     @pl.loop(0, GROUPS)
     def _(j):
-        merge_gu(2, wu_hbm, wu, ul, ur, j)
+        merge_gu(2, wu_hbm, wu, ult, ur, j)
 
     n_y = spread(nby, y, at_y, 12)
     start(n_y)
@@ -167,7 +171,7 @@
     sqd = sqd_x[0] + sqd_x[1] + sqd_x[2] + sqd_x[3]
     normd = jnp.sqrt(sqd + EPS)
     scd[0:1] = normd
-    scd[1:2] = dmag[...] / normd
+    scd[1:2] = dmag[...].reshape(1, 512) / normd
     g_own[2].wait()
     wait(g_fwd[2:])
     g_last.wait()
@@ -182,7 +186,8 @@
         zt[0, b * 32 : b * 32 + 32] = v
         zt[1, p * 32 : p * 32 + 32] = v
 
-    pry[y, 0:32] = nt(lt[...], xt[0]).astype(BF16)
+    pry[y, 0:16] = nt(glt[...], xt[0]).astype(BF16)
+    pry[y, 16:32] = nt(ult[...], xt[0]).astype(BF16)
     pry[y, 32:48] = nt(dr[...], zt[0]).astype(BF16)
     p_y = spread(pry, y, at_y, 18)
     start(p_y)
@@ -314,7 +319,7 @@
                     nbz[0, k : k + 1] + nbz[1, k : k + 1] + nbz[2, k : k + 1] + nbz[3, k : k + 1] + EPS
                 )
                 nrm[k : k + 1] = n
-                scl[k : k + 1] = mag[...] / n
+                scl[k : k + 1] = mag[...].reshape(1, 3584) / n
 
         @pl.when(t == 7)
         def _():
@@ -417,7 +422,6 @@
     f = jax.ShapeDtypeStruct
     V = pltpu.VMEM
     G, C = GROUPS, HALF
-    lt = jnp.concatenate([gl.T, ul.T], axis=0)
     call = pl.pallas_call(
         kernel,
         out_shape=(
@@ -426,7 +430,7 @@
             f((16, 3584), F32), f((16, 512), F32), f((16, 3584), F32), f((16, 512), F32),
             f((16, 512), F32), f((16, 3584), F32),
         ),
-        in_specs=[vm, vm, hbm, hbm, hbm] + [vm] * 11,
+        in_specs=[vm, vm, hbm, hbm, hbm] + [vm] * 9,
         out_specs=(vm,) * 11,
         scratch_shapes=[
             V((G, 2, 512, C), BF16), V((G, 2, 512, C), BF16), V((G, 2, C, 512), BF16),
@@ -455,14 +459,23 @@
             collective_id=0, has_side_effects=True, vmem_limit_bytes=63 * 1024 * 1024
         ),
     )
-    o, d, ggm, gum, gdm, ggr, ggl, gur, gul, gdr, gdl = call(
-        tok, cot, fg, fu, fd, gl, gr, ul, ur, dl, dr, lt, dl.T,
-        gmag.reshape(1, -1), umag.reshape(1, -1), dmag.reshape(1, -1),
-    )
-    return (
-        o, d, ggm.reshape(-1), gum.reshape(-1), gdm.reshape(-1),
-        ggr, ggl.T, gur, gul.T, gdr, gdl.T,
-    )
+    res = call(tok, cot, fg, fu, fd, gl.T, gr, ul.T, ur, dl.T, dr, gmag, umag, dmag)
+    flat = (2, 3, 4)
+
+    def finish(*refs):
+        for k in range(11):
+            value = refs[k][...]
+            refs[k + 11][...] = value.reshape(-1) if k in flat else value
+
+    o, d, ggm, gum, gdm, ggr, ggl, gur, gul, gdr, gdl = pl.pallas_call(
+        finish,
+        out_shape=tuple(
+            f((r.size,) if k in flat else r.shape, r.dtype) for k, r in enumerate(res)
+        ),
+        in_specs=[vm] * 11,
+        out_specs=(vm,) * 11,
+    )(*res)
+    return o, d, ggm, gum, gdm, ggr, ggl.T, gur, gul.T, gdr, gdl.T
 
 
 def solution(mesh):

time: 187 us -> 164 us (0.88)
  local copies, waits for them, and re-layouts: 21 us -> 0 us
  other arithmetic: 4.06 us -> 0 us
  Pallas kernels: 159 us -> 161 us
    unnamed x12 -> x0, local copies, waits for them, and re-layouts: 18.3 us -> none
    pallas_call x1 -> x2, Pallas kernels: 159 us -> 161 us  [the longest x1 159 us: per_device(): call(tok, cot, fg, fu, fd, gl.T, gr, ul.T, ur, dl.T, dr, gmag, umag, dmag)]
    pallas_call x2 -> x0, other arithmetic: 2.71 us -> none  [per_device(): call(tok, cot, fg, fu, fd, gl, gr, ul, ur, dl, dr, lt, dl.T, gmag.reshape...]
    reshape x2 -> x0, local copies, waits for them, and re-layouts: 2.65 us -> none  [the longest x1 1.33 us: per_device(): gmag.reshape(1, -1)]
where the time goes in v2:
time: 164 us; the launch traced here: 162 us
  Pallas kernels  161 us (98%)
    pallas_call x1, Pallas kernels, per_device(): call(tok, cot, fg, fu, fd, gl.T, gr, ul.T, ur, dl.T, dr, gmag, umag, dmag)  159 us

profile of v2, /device:TPU:1, one launch (start us, length us, event | category | flops | bytes accessed | tf_op | source)
XLA Modules:
  0.0 162.0 jit_solution(17650188685431865264)
XLA Ops:
  0.6 159.1 %shard_map.221 = (bf16[64,512]{1,0:T(8,128)(2,1)}, bf16[64,512]{1,0:T(8,128)(2,1)}, f32[1,3584]{1,0:T(1,128)}, f32[1,3584]{1,0:T(1,128)}, f32[1,512]{1,0:T(1,128...) custom-call(bf16[64,512]{1,0:T(8,128)(2,1)} %tok.1, ...), custom_call_target="tpu_custom_call" | custom-call | tf_op jit(solution)/shard_map/pallas_call | solution.py:462
  159.8 2.3 %shard_map.222 = (bf16[64,512]{1,0:T(8,128)(2,1)}, bf16[64,512]{1,0:T(8,128)(2,1)}, f32[3584]{0:T(1024)}, f32[3584]{0:T(1024)}, f32[512]{0:T(512)}, /*index=5*/f...) custom-call(bf16[64,512]{1,0:T(8,128)(2,1)} %get-tuple-element.33.re, ...), custom_call_target="tpu_custom_call" | custom-call | tf_op jit(solution)/shard_map/pallas_call | solution.py:470

commit v3 on v2

--- a/solution.py
+++ b/solution.py
@@ -33,7 +33,7 @@
     wg, wu, wd, gath, xt, zt, sqd_c, sqd_x, scd, nby, nbz, scl, nrm, pry, prz, pr,
     part, r1h, r1f, q, r2h, r2f, hz, mgy, mgz, oacc, xacc, bk,
     fs, fr, th, tf, smc, smx, mdc, mdx,
-    wsem, ssem, rsem, ms, mr,
+    wsem, ssem, rsem, ms, mr, spread_s, spread_r,
 ):
     dp = lax.axis_index("dp")
     mp = lax.axis_index("mp")
@@ -59,10 +59,35 @@
     def mcopy(src, dst, k, dev):
         return rcopy(src, dst, ms.at[k], mr.at[k], dev)
 
+    def landed(ref, sem):
+        pltpu.make_async_copy(ref, ref, sem).wait()
+
     def spread(slots, me, place, k):
-        return [
-            mcopy(slots.at[me], slots.at[me], k + d - 1, place((me + d) % 4)) for d in (1, 2, 3)
-        ]
+        for d in (1, 2, 3):
+            rcopy(
+                slots.at[me], slots.at[me], spread_s.at[k], spread_r.at[k], place((me + d) % 4)
+            ).start()
+
+    def spread_wait(slots, k):
+        landed(slots.at[0:3], spread_s.at[k])
+        landed(slots.at[0:3], spread_r.at[k])
+
+    def ring_own(slots, me, place, k):
+        for i in ((me + 1) % 4, (me + 3) % 4):
+            rcopy(slots.at[me], slots.at[me], spread_s.at[k], spread_r.at[k], place(i)).start()
+
+    def ring_pass(slots, me, place, k):
+        landed(slots.at[0:2], spread_s.at[k])
+        landed(slots.at[0:2], spread_r.at[k])
+        half = slots.shape[2] // 2
+        right, left = (me + 1) % 4, (me + 3) % 4
+        a, b = slots.at[left, :, 0:half], slots.at[right, :, half:]
+        rcopy(a, a, spread_s.at[k + 1], spread_r.at[k + 1], place(right)).start()
+        rcopy(b, b, spread_s.at[k + 1], spread_r.at[k + 1], place(left)).start()
+
+    def ring_wait(slots, k):
+        landed(slots.at[0], spread_s.at[k + 1])
+        landed(slots.at[0], spread_r.at[k + 1])
 
     def start(copies):
         for cp in copies:
@@ -76,14 +101,14 @@
         return pltpu.make_async_copy(
             wd_hbm.at[pl.ds(pl.multiple_of((j * 2 + h) * HALF, HALF), HALF)],
             wd.at[j, h],
-            wsem.at[0, j, h],
+            wsem.at[0, j],
         )
 
     def load_gu(w_hbm, w, k, j, h):
         return pltpu.make_async_copy(
             w_hbm.at[:, pl.ds(pl.multiple_of((j * 2 + h) * HALF, HALF), HALF)],
             w.at[j, h],
-            wsem.at[k, j, h],
+            wsem.at[k, j],
         )
 
     @pl.loop(0, GROUPS)
@@ -117,8 +142,8 @@
     start(g_own)
 
     def merge_down(j, total):
+        landed(wd.at[j], wsem.at[0, j])
         for h in (0, 1):
-            load_d(j, h).wait()
             rows = pl.ds(pl.multiple_of((j * 2 + h) * HALF, HALF), HALF)
             m = wd[j, h].astype(F32) + tn(dlt[:, rows], dr[...])
             wd[j, h] = m.astype(BF16)
@@ -139,35 +164,25 @@
     ]
     start(g_fwd)
 
-    def merge_gu(k, w_hbm, w, left, right, j):
-        for h in (0, 1):
-            load_gu(w_hbm, w, k, j, h).wait()
-            cols = pl.ds(pl.multiple_of((j * 2 + h) * HALF, HALF), HALF)
-            m = w[j, h].astype(F32) + tn(left[...], right[:, cols])
-            w[j, h] = m.astype(BF16)
-            nby[y, k - 1 : k, cols] = jnp.sum(m * m, axis=0, keepdims=True)
-
-    @pl.loop(0, GROUPS)
-    def _(j):
-        merge_gu(1, wg_hbm, wg, glt, gr, j)
+    def merge_gu(j):
+        for k, w, left, right in ((0, wg, glt, gr), (1, wu, ult, ur)):
+            landed(w.at[j], wsem.at[k + 1, j])
+            for h in (0, 1):
+                cols = pl.ds(pl.multiple_of((j * 2 + h) * HALF, HALF), HALF)
+                m = w[j, h].astype(F32) + tn(left[...], right[:, cols])
+                w[j, h] = m.astype(BF16)
+                nby[y, k : k + 1, cols] = jnp.sum(m * m, axis=0, keepdims=True)
 
     s_core.wait()
     sqd_x[x] = sqd_c[0] + sqd_c[1]
-    s_x = spread(sqd_x, x, at_x, 8)
-    start(s_x)
+    spread(sqd_x, x, at_x, 0)
     wait(g_fwd[:2])
     oo = gath.at[xo, c]
-    g_last = mcopy(oo, oo, 11, other)
+    g_last = mcopy(oo, oo, 8, other)
     g_last.start()
-
-    @pl.loop(0, GROUPS)
-    def _(j):
-        merge_gu(2, wu_hbm, wu, ult, ur, j)
-
-    n_y = spread(nby, y, at_y, 12)
-    start(n_y)
-
-    wait(s_x)
+    merge_gu(0)
+
+    spread_wait(sqd_x, 0)
     sqd = sqd_x[0] + sqd_x[1] + sqd_x[2] + sqd_x[3]
     normd = jnp.sqrt(sqd + EPS)
     scd[0:1] = normd
@@ -186,24 +201,11 @@
         zt[0, b * 32 : b * 32 + 32] = v
         zt[1, p * 32 : p * 32 + 32] = v
 
-    pry[y, 0:16] = nt(glt[...], xt[0]).astype(BF16)
-    pry[y, 16:32] = nt(ult[...], xt[0]).astype(BF16)
-    pry[y, 32:48] = nt(dr[...], zt[0]).astype(BF16)
-    p_y = spread(pry, y, at_y, 18)
-    start(p_y)
-    n_z = spread(nbz, z, at_z, 15)
-    p_z = spread(prz, z, at_z, 21)
-    m_y = spread(mgy, y, at_y, 24)
-    m_z = spread(mgz, z, at_z, 27)
-
-    ri = lax.broadcasted_iota(jnp.int32, (512, 512), 0)
-    ci = lax.broadcasted_iota(jnp.int32, (512, 512), 1)
-    swapped = ((ri // 32) % 4) * 128 + (ri // 128) * 32 + ri % 32
-    swap = (swapped == ci).astype(BF16)
-
-    oacc[...] = jnp.zeros_like(oacc)
-    xacc[...] = jnp.zeros_like(xacc)
-    bk[...] = jnp.zeros_like(bk)
+    def swap():
+        ri = lax.broadcasted_iota(jnp.int32, (512, 512), 0)
+        ci = lax.broadcasted_iota(jnp.int32, (512, 512), 1)
+        swapped = ((ri // 32) % 4) * 128 + (ri // 128) * 32 + ri % 32
+        return (swapped == ci).astype(BF16)
 
     def geometry(h):
         ia = y + h * (z - y)
@@ -248,9 +250,17 @@
         else:
             dr_, dl_ = at_b(br), at_b(bl)
         return [
-            rcopy(*a, ssem.at[s, j, h, 0], rsem.at[s, j, h, 0], dr_),
-            rcopy(*b, ssem.at[s, j, h, 1], rsem.at[s, j, h, 1], dl_),
+            rcopy(*a, ssem.at[s, j % 3, h], rsem.at[s, j % 3, h], dr_),
+            rcopy(*b, ssem.at[s, j % 3, h], rsem.at[s, j % 3, h], dl_),
         ]
+
+    def arrived(s, j, h):
+        both = (
+            r1h.at[j, h], r1f.at[j, h], r2h.at[j, h], r2f.at[j, h],
+            hz.at[j, h, :, 0, 0:2], hz.at[j, h, :, 0, 0], hz.at[j, h, :, 0:2], hz.at[j, h, :, 0],
+        )[s]
+        landed(both, ssem.at[s, j % 3, h])
+        landed(both, rsem.at[s, j % 3, h])
 
     def add_into(ref, extra):
         ref[...] = (ref[...].astype(F32) + extra[...].astype(F32)).astype(BF16)
@@ -261,7 +271,7 @@
         br, bl = (ib + 1) % 4, (ib + 3) % 4
         cols = pl.ds(pl.multiple_of((j * 2 + h) * HALF, HALF), HALF)
         if s > 0:
-            wait(copies(s - 1, j, h))
+            arrived(s - 1, j, h)
         if s == 0:
             part[j, h, 0] = nn(xt[h], wg[j, h]).astype(BF16).reshape(4, 4, 32, HALF)
             part[j, h, 1] = nn(xt[h], wu[j, h]).astype(BF16).reshape(4, 4, 32, HALF)
@@ -311,25 +321,18 @@
 
     @pl.loop(0, GROUPS + STAGES - 1)
     def _(t):
-        @pl.when(t == 4)
-        def _():
-            wait(n_z)
-            for k, mag in enumerate((gmag, umag)):
-                n = jnp.sqrt(
-                    nbz[0, k : k + 1] + nbz[1, k : k + 1] + nbz[2, k : k + 1] + nbz[3, k : k + 1] + EPS
-                )
-                nrm[k : k + 1] = n
-                scl[k : k + 1] = mag[...].reshape(1, 3584) / n
-
-        @pl.when(t == 7)
-        def _():
-            wait(p_z)
-            total = sum(prz[k].astype(F32) for k in range(4)).astype(BF16)
-            pr[0] = total
-            pr[1] = nn(total, swap).astype(BF16)
-
         for s in range(STAGES):
             j = t - s
+            if s == 4:
+
+                @pl.when(t == 4)
+                def _():
+                    spread_wait(nbz, 2)
+                    for k, mag in enumerate((gmag, umag)):
+                        row = slice(k, k + 1)
+                        n = jnp.sqrt(nbz[0, row] + nbz[1, row] + nbz[2, row] + nbz[3, row] + EPS)
+                        nrm[row] = n
+                        scl[row] = mag[...].reshape(1, 3584) / n
 
             @pl.when(jnp.logical_and(j >= 0, j < GROUPS))
             def _():
@@ -337,27 +340,66 @@
                 def _(h):
                     stage(s, j, h)
 
-        @pl.when(t == 0)
-        def _():
-            wait(n_y)
+        @pl.when(t < 3)
+        def _():
+            merge_gu(2 * t + 1)
+            merge_gu(2 * t + 2)
+
+        @pl.when(t == 1)
+        def _():
+            pry[y, 0:16] = nt(glt[...], xt[0]).astype(BF16)
+            pry[y, 16:32] = nt(ult[...], xt[0]).astype(BF16)
+            pry[y, 32:48] = nt(dr[...], zt[0]).astype(BF16)
+            ring_own(pry, y, at_y, 3)
+
+        @pl.when(t == 2)
+        def _():
+            spread(nby, y, at_y, 1)
+            ring_pass(pry, y, at_y, 3)
+
+        @pl.when(t == 3)
+        def _():
+            oacc[...] = jnp.zeros_like(oacc)
+            xacc[...] = jnp.zeros_like(xacc)
+            bk[...] = jnp.zeros_like(bk)
+            spread_wait(nby, 1)
             nbz[z] = nby[0] + nby[1] + nby[2] + nby[3]
-            start(n_z)
-
-        @pl.when(t == 1)
-        def _():
-            wait(p_y)
+            spread(nbz, z, at_z, 2)
+
+        @pl.when(t == 4)
+        def _():
+            ring_wait(pry, 3)
             prz[z] = sum(pry[k].astype(F32) for k in range(4)).astype(BF16)
-            start(p_z)
+            ring_own(prz, z, at_z, 5)
+
+        @pl.when(t == 5)
+        def _():
+            ring_pass(prz, z, at_z, 5)
+
+        @pl.when(t == 6)
+        def _():
+            ring_wait(prz, 5)
+            total = sum(prz[k].astype(F32) for k in range(4)).astype(BF16)
+            pr[0] = total
+            pr[1] = nn(total, swap()).astype(BF16)
 
         @pl.when(t == GROUPS + 3)
         def _():
-            start(m_y)
+            ring_own(mgy, y, at_y, 7)
+
+        @pl.when(t == GROUPS + 4)
+        def _():
+            ring_pass(mgy, y, at_y, 7)
 
         @pl.when(t == GROUPS + 5)
         def _():
-            wait(m_y)
+            ring_wait(mgy, 7)
             mgz[z] = mgy[0] + mgy[1] + mgy[2] + mgy[3]
-            start(m_z)
+            ring_own(mgz, z, at_z, 9)
+
+        @pl.when(t == GROUPS + 6)
+        def _():
+            ring_pass(mgz, z, at_z, 9)
 
     md = jnp.zeros((1, 512), F32)
     for b in range(16):
@@ -368,47 +410,46 @@
         md = md + jnp.sum(o * gath[px, pc, 1, rows].astype(F32), axis=0, keepdims=True)
         fs[pc, 0, px, rows] = o.astype(BF16)
         fs[pc, 1, px, rows] = v.astype(BF16)
-    f_core = mcopy(fs.at[1 - c], fr, 30, other)
+    f_core = mcopy(fs.at[1 - c], fr, 9, other)
     f_core.start()
     mdc[c] = md
-    smc[c] = (bk[0] + nn(bk[1].astype(BF16), swap)).astype(BF16)
-    md_core = mcopy(mdc.at[c], mdc.at[c], 31, other)
-    sm_core = mcopy(smc.at[c], smc.at[c], 32, other)
+    smc[c] = (bk[0] + nn(bk[1].astype(BF16), swap())).astype(BF16)
+    md_core = mcopy(mdc.at[c], mdc.at[c], 10, other)
+    sm_core = mcopy(smc.at[c], smc.at[c], 11, other)
     start([md_core, sm_core])
     f_core.wait()
     add_into(fs.at[c], fr)
     f_half = [
-        mcopy(fs.at[c, :, xo, 0:32], th.at[0], 33, at_x(xr)),
-        mcopy(fs.at[c, :, xo, 32:64], th.at[1], 34, at_x(xl)),
+        mcopy(fs.at[c, :, xo, 0:32], th.at[0], 12, at_x(xr)),
+        mcopy(fs.at[c, :, xo, 32:64], th.at[1], 13, at_x(xl)),
     ]
     start(f_half)
     wait([md_core, sm_core])
     mdx[x] = mdc[0] + mdc[1]
     smx[x] = (smc[0].astype(F32) + smc[1].astype(F32)).astype(BF16)
-    sm_x = spread(smx, x, at_x, 37)
-    md_x = spread(mdx, x, at_x, 40)
-    start(sm_x)
-    start(md_x)
+    ring_own(smx, x, at_x, 11)
+    spread(mdx, x, at_x, 13)
     wait(f_half)
     add_into(fs.at[c, :, xr, 0:32], th.at[0])
     add_into(fs.at[c, :, xl, 32:64], th.at[1])
     f_full = [
-        mcopy(fs.at[c, :, xr], tf.at[0], 35, at_x(xr)),
-        mcopy(fs.at[c, :, xl], tf.at[1], 36, at_x(xl)),
+        mcopy(fs.at[c, :, xr], tf.at[0], 14, at_x(xr)),
+        mcopy(fs.at[c, :, xl], tf.at[1], 15, at_x(xl)),
     ]
     start(f_full)
-
-    wait(m_z)
+    ring_pass(smx, x, at_x, 11)
+
+    ring_wait(mgz, 9)
     mags = (mgz[0] + mgz[1] + mgz[2] + mgz[3]) / nrm[...]
     ggm[...] = mags[0:1]
     gum[...] = mags[1:2]
-    wait(sm_x)
+    ring_wait(smx, 11)
     back = sum(smx[k].astype(F32) for k in range(4)).astype(BF16)
     lg = nn(back[0:32], xt[0])
     ggl[...] = lg[0:16]
     gul[...] = lg[16:32]
     gdr[...] = nn(back[32:48], zt[0])
-    wait(md_x)
+    spread_wait(mdx, 13)
     gdm[...] = (mdx[0] + mdx[1] + mdx[2] + mdx[3]) / scd[0:1]
     wait(f_full)
     tot = fs[c, :, x].astype(F32) + tf[0].astype(F32) + tf[1].astype(F32)
@@ -449,11 +490,13 @@
             V((2, 2, 32, 512), BF16), V((2, 2, 64, 512), BF16),
             V((2, 48, 512), BF16), V((4, 48, 512), BF16),
             V((2, 1, 512), F32), V((4, 1, 512), F32),
-            pltpu.SemaphoreType.DMA((3, G, 2)),
-            pltpu.SemaphoreType.DMA((8, G, 2, 2)),
-            pltpu.SemaphoreType.DMA((8, G, 2, 2)),
-            pltpu.SemaphoreType.DMA((43,)),
-            pltpu.SemaphoreType.DMA((43,)),
+            pltpu.SemaphoreType.DMA((3, G)),
+            pltpu.SemaphoreType.DMA((8, 3, 2)),
+            pltpu.SemaphoreType.DMA((8, 3, 2)),
+            pltpu.SemaphoreType.DMA((16,)),
+            pltpu.SemaphoreType.DMA((16,)),
+            pltpu.SemaphoreType.DMA((14,)),
+            pltpu.SemaphoreType.DMA((14,)),
         ],
         compiler_params=pltpu.CompilerParams(
             collective_id=0, has_side_effects=True, vmem_limit_bytes=63 * 1024 * 1024

time: 164 us -> 156 us (0.951)
  Pallas kernels: 161 us -> 154 us
    pallas_call x1, Pallas kernels: 159 us -> 152 us  [per_device(): call(tok, cot, fg, fu, fd, gl.T, gr, ul.T, ur, dl.T, dr, gmag, umag, dmag)]
where the time goes in v3:
time: 156 us; the launch traced here: 155 us
  Pallas kernels  154 us (99%)
    pallas_call x1, Pallas kernels, per_device(): call(tok, cot, fg, fu, fd, gl.T, gr, ul.T, ur, dl.T, dr, gmag, umag, dmag)  152 us

profile of v3, /device:TPU:1, one launch (start us, length us, event | category | flops | bytes accessed | tf_op | source)
XLA Modules:
  0.0 155.1 jit_solution(17460191209441056870)
XLA Ops:
  0.6 152.2 %shard_map.221 = (bf16[64,512]{1,0:T(8,128)(2,1)}, bf16[64,512]{1,0:T(8,128)(2,1)}, f32[1,3584]{1,0:T(1,128)}, f32[1,3584]{1,0:T(1,128)}, f32[1,512]{1,0:T(1,128...) custom-call(bf16[64,512]{1,0:T(8,128)(2,1)} %tok.1, ...), custom_call_target="tpu_custom_call" | custom-call | tf_op jit(solution)/shard_map/pallas_call | solution.py:505
  152.9 2.3 %shard_map.222 = (bf16[64,512]{1,0:T(8,128)(2,1)}, bf16[64,512]{1,0:T(8,128)(2,1)}, f32[3584]{0:T(1024)}, f32[3584]{0:T(1024)}, f32[512]{0:T(512)}, /*index=5*/f...) custom-call(bf16[64,512]{1,0:T(8,128)(2,1)} %get-tuple-element.33.re, ...), custom_call_target="tpu_custom_call" | custom-call | tf_op jit(solution)/shard_map/pallas_call | solution.py:513

commit v4 on v3

v4 whole, which is shorter than its diff:
```python
import jax
import jax.numpy as jnp
from jax import lax
from jax.experimental import pallas as pl
from jax.experimental.pallas import tpu as pltpu
from jax.sharding import PartitionSpec as P

F32 = jnp.float32
BF16 = jnp.bfloat16
MESH = pl.DeviceIdType.MESH
EPS = 1e-06

GROUPS = 7
HALF = 256
STAGES = 9


def nn(a, b):
    return jnp.dot(a, b, preferred_element_type=F32)


def nt(a, b):
    return lax.dot_general(a, b, (((1,), (1,)), ((), ())), preferred_element_type=F32)


def tn(a, b):
    return lax.dot_general(a, b, (((0,), (0,)), ((), ())), preferred_element_type=F32)


def kernel(
    tok, cot, wg_hbm, wu_hbm, wd_hbm, glt, gr, ult, ur, dlt, dr, gmag, umag, dmag,
    out, dx, ggm, gum, gdm, ggr, ggl, gur, gul, gdr, gdl,
    wg, wu, wd, gath, zt, sqd_c, sqd_x, scd, nf, nby, nbz, scl, nrm, lpad, dpad, pry, prz, pd, pr,
    part, r1h, r1f, q, r2h, r2f, hz, mf, mgy, mgz, oacc, xacc, bk,
    fs, fr, th, tf, smd, smy, back, mdc, mdx,
    wsem, ssem, rsem, ms, mr, spread_s, spread_r,
):
    dp = lax.axis_index("dp")
    mp = lax.axis_index("mp")
    x, c = dp // 2, dp % 2
    y, z = mp // 4, mp % 4

    def at_x(i):
        return (i * 2 + c, mp)

    def at_y(i):
        return (dp, i * 4 + z)

    def at_z(i):
        return (dp, y * 4 + i)

    def at_x_other(i):
        return (i * 2 + 1 - c, mp)

    other = at_x_other(x)

    def rcopy(src, dst, s, r, dev):
        return pltpu.make_async_remote_copy(
            src_ref=src, dst_ref=dst, send_sem=s, recv_sem=r, device_id=dev, device_id_type=MESH
        )

    def mcopy(src, dst, k, dev):
        return rcopy(src, dst, ms.at[k], mr.at[k], dev)

    def landed(ref, sem):
        pltpu.make_async_copy(ref, ref, sem).wait()

    def spread(slots, me, place, k):
        for d in (1, 2, 3):
            rcopy(
                slots.at[me], slots.at[me], spread_s.at[k], spread_r.at[k], place((me + d) % 4)
            ).start()

    def spread_wait(slots, k):
        landed(slots.at[0:3], spread_s.at[k])
        landed(slots.at[0:3], spread_r.at[k])

    def ring_own(slots, me, place, k):
        for i in ((me + 1) % 4, (me + 3) % 4):
            rcopy(slots.at[me], slots.at[me], spread_s.at[k], spread_r.at[k], place(i)).start()

    def ring_pass(slots, me, place, k):
        landed(slots.at[0:2], spread_s.at[k])
        landed(slots.at[0:2], spread_r.at[k])
        axis = 2 if slots.shape[2] > 128 else 1
        half = slots.shape[axis] // 2
        right, left = (me + 1) % 4, (me + 3) % 4
        if axis == 2:
            a, b = slots.at[left, :, 0:half], slots.at[right, :, half:]
        else:
            a, b = slots.at[left, 0:half], slots.at[right, half:]
        rcopy(a, a, spread_s.at[k + 1], spread_r.at[k + 1], place(right)).start()
        rcopy(b, b, spread_s.at[k + 1], spread_r.at[k + 1], place(left)).start()

    def ring_wait(slots, k):
        landed(slots.at[0], spread_s.at[k + 1])
        landed(slots.at[0], spread_r.at[k + 1])

    def start(copies):
        for cp in copies:
            cp.start()

    def wait(copies):
        for cp in copies:
            cp.wait()

    def load_d(j, h):
        return pltpu.make_async_copy(
            wd_hbm.at[pl.ds(pl.multiple_of((j * 2 + h) * HALF, HALF), HALF)],
            wd.at[j, h],
            wsem.at[0, j],
        )

    def load_gu(w_hbm, w, k, j, h):
        return pltpu.make_async_copy(
            w_hbm.at[:, pl.ds(pl.multiple_of((j * 2 + h) * HALF, HALF), HALF)],
            w.at[j, h],
            wsem.at[k, j],
        )

    @pl.loop(0, GROUPS)
    def _(j):
        for h in (0, 1):
            load_d(j, h).start()

    @pl.loop(0, GROUPS)
    def _(j):
        for h in (0, 1):
            load_gu(wg_hbm, wg, 1, j, h).start()
            load_gu(wu_hbm, wu, 2, j, h).start()

    gath[0, x, c] = tok[...]
    gath[1, x, c] = cot[...]

    barrier = pltpu.get_barrier_semaphore()
    for d in (1, 2, 3):
        for dev in (at_x((x + d) % 4), at_y((y + d) % 4), at_z((z + d) % 4)):
            pl.semaphore_signal(barrier, inc=1, device_id=dev, device_id_type=MESH)
    for dev in (other, *(at_x_other((x + d) % 4) for d in (1, 2, 3))):
        pl.semaphore_signal(barrier, inc=1, device_id=dev, device_id_type=MESH)
    pl.semaphore_wait(barrier, 13)

    xr, xl, xo = (x + 1) % 4, (x + 3) % 4, (x + 2) % 4
    own = gath.at[:, x, c]
    g_own = [
        mcopy(own, own, 0, at_x(xr)),
        mcopy(own, own, 1, at_x(xl)),
        mcopy(own, own, 2, other),
    ]
    start(g_own)

    def merge_down(j, total):
        landed(wd.at[j], wsem.at[0, j])
        for h in (0, 1):
            rows = pl.ds(pl.multiple_of((j * 2 + h) * HALF, HALF), HALF)
            m = wd[j, h].astype(F32) + tn(dlt[:, rows], dr[...])
            wd[j, h] = m.astype(BF16)
            total = total + jnp.sum(m * m, axis=0, keepdims=True)
        return total

    sqd_c[c] = lax.fori_loop(0, GROUPS, merge_down, jnp.zeros((1, 512), F32))
    s_core = mcopy(sqd_c.at[c], sqd_c.at[c], 3, other)
    s_core.start()

    wait(g_own[:2])
    lo, ro = gath.at[:, xl, c], gath.at[:, xr, c]
    a, b = gath.at[:, xl, c, 0:32], gath.at[:, xr, c, 32:64]
    g_fwd = [
        mcopy(a, a, 4, at_x(xr)),
        mcopy(b, b, 5, at_x(xl)),
        mcopy(a, a, 6, at_x_other(xr)),
        mcopy(b, b, 7, at_x_other(xl)),
        mcopy(lo, lo, 8, other),
        mcopy(ro, ro, 16, other),
    ]
    start(g_fwd)

    def merge_gu(j):
        for k, w, left, right in ((0, wg, glt, gr), (1, wu, ult, ur)):
            landed(w.at[j], wsem.at[k + 1, j])
            for h in (0, 1):
                cols = pl.ds(pl.multiple_of((j * 2 + h) * HALF, HALF), HALF)
                m = w[j, h].astype(F32) + tn(left[...], right[:, cols])
                w[j, h] = m.astype(BF16)
                nf[pl.ds(k * 8 + j, 1), h * HALF : (h + 1) * HALF] = jnp.sum(m * m, axis=0, keepdims=True)

    s_core.wait()
    sqd_x[x] = sqd_c[0] + sqd_c[1]
    spread(sqd_x, x, at_x, 0)
    merge_gu(0)

    spread_wait(sqd_x, 0)
    sqd = sqd_x[0] + sqd_x[1] + sqd_x[2] + sqd_x[3]
    normd = jnp.sqrt(sqd + EPS)
    scd[0:1] = normd
    scd[1:2] = dmag[...].reshape(1, 512) / normd
    g_own[2].wait()
    wait(g_fwd)

    nf[7:8] = jnp.ones((1, 512), F32)
    nf[15:16] = jnp.ones((1, 512), F32)
    scl[...] = jnp.ones_like(scl)
    mf[...] = jnp.zeros_like(mf)

    def tokens():
        return gath[0].reshape(512, 512)

    zt[...] = (gath[1].reshape(512, 512).astype(F32) * scd[1:2]).astype(BF16)

    def geometry(h):
        ia = y + h * (z - y)
        ib = z + h * (y - z)

        def at_a(i):
            return (dp, (i + h * (y - i)) * 4 + z + h * (i - z))

        def at_b(i):
            return (dp, (y + h * (i - y)) * 4 + i + h * (z - i))

        return ia, ib, at_a, at_b

    def copies(s, j, h):
        ia, ib, at_a, at_b = geometry(h)
        ar, al, ao = (ia + 1) % 4, (ia + 3) % 4, (ia + 2) % 4
        br, bl, bo = (ib + 1) % 4, (ib + 3) % 4, (ib + 2) % 4
        if s == 0:
            a = part.at[j, h, :, ao, 0:2], r1h.at[j, h, 0]
            b = part.at[j, h, :, ao, 2:4], r1h.at[j, h, 1]
        elif s == 1:
            a = part.at[j, h, :, ar], r1f.at[j, h, 0]
            b = part.at[j, h, :, al], r1f.at[j, h, 1]
        elif s == 2:
            a = q.at[j, h, :, bo, 0:16], r2h.at[j, h, 0]
            b = q.at[j, h, :, bo, 16:32], r2h.at[j, h, 1]
        elif s == 3:
            a = q.at[j, h, :, br], r2f.at[j, h, 0]
            b = q.at[j, h, :, bl], r2f.at[j, h, 1]
        elif s == 4:
            a = b = (hz.at[j, h, :, ia, ib],) * 2
        elif s == 5:
            a = (hz.at[j, h, :, ia, bl, 0:16],) * 2
            b = (hz.at[j, h, :, ia, br, 16:32],) * 2
        elif s == 6:
            a = b = (hz.at[j, h, :, ia],) * 2
        else:
            a = (hz.at[j, h, :, al, 0:2],) * 2
            b = (hz.at[j, h, :, ar, 2:4],) * 2
        if s in (0, 1, 6, 7):
            dr_, dl_ = at_a(ar), at_a(al)
        else:
            dr_, dl_ = at_b(br), at_b(bl)
        return [
            rcopy(*a, ssem.at[s, j % 2, h], rsem.at[s, j % 3, h], dr_),
            rcopy(*b, ssem.at[s, j % 2, h], rsem.at[s, j % 3, h], dl_),
        ]

    def arrived(s, j, h):
        both = (
            r1h.at[j, h], r1f.at[j, h], r2h.at[j, h], r2f.at[j, h],
            hz.at[j, h, :, 0, 0:2], hz.at[j, h, :, 0, 0], hz.at[j, h, :, 0:2], hz.at[j, h, :, 0],
        )[s]
        landed(both, ssem.at[s, j % 2, h])
        landed(both, rsem.at[s, j % 3, h])

    def add_into(ref, extra):
        ref[...] = (ref[...].astype(F32) + extra[...].astype(F32)).astype(BF16)

    def stage(s, j, h):
        ia, ib, _, _ = geometry(h)
        ar, al = (ia + 1) % 4, (ia + 3) % 4
        br, bl = (ib + 1) % 4, (ib + 3) % 4
        cols = pl.ds(pl.multiple_of((j * 2 + h) * HALF, HALF), HALF)
        if 0 < s < 9:
            arrived(s - 1, j, h)
        if s == 0:
            part[j, h, 0] = nn(tokens(), wg[j, h]).astype(BF16).reshape(4, 4, 32, HALF)
            part[j, h, 1] = nn(tokens(), wu[j, h]).astype(BF16).reshape(4, 4, 32, HALF)
            part[j, h, 2] = nt(zt[...], wd[j, h]).astype(BF16).reshape(4, 4, 32, HALF)
        elif s == 1:
            add_into(part.at[j, h, :, ar, 0:2], r1h.at[j, h, 0])
            add_into(part.at[j, h, :, al, 2:4], r1h.at[j, h, 1])
        elif s == 2:
            q[j, h] = (
                part[j, h, :, ia].astype(F32)
                + r1f[j, h, 0].astype(F32)
                + r1f[j, h, 1].astype(F32)
            ).astype(BF16)
        elif s == 3:
            add_into(q.at[j, h, :, br, 0:16], r2h.at[j, h, 0])
            add_into(q.at[j, h, :, bl, 16:32], r2h.at[j, h, 1])
        elif s == 4:
            pg, pu, gh = (
                q[j, h, k, ib].astype(F32) + r2f[j, h, 0, k].astype(F32) + r2f[j, h, 1, k].astype(F32)
                for k in range(3)
            )
            local = pl.ds(pl.multiple_of(h * HALF, HALF), HALF)
            sg, su = scl[pl.ds(j, 1), local], scl[pl.ds(8 + j, 1), local]
            ga, ua = pg * sg, pu * su
            sig = 1.0 / (1.0 + jnp.exp(-ga))
            silu = ga * sig
            dg = gh * ua * sig * (1.0 + ga * (1.0 - sig))
            du = gh * silu
            hz[j, h, 0, ia, ib] = (silu * ua).astype(BF16)
            hz[j, h, 1, ia, ib] = (dg * sg).astype(BF16)
            hz[j, h, 2, ia, ib] = (du * su).astype(BF16)
            mf[pl.ds(j, 1), local] = jnp.sum(dg * pg, axis=0, keepdims=True)
            mf[pl.ds(8 + j, 1), local] = jnp.sum(du * pu, axis=0, keepdims=True)
        elif s == 8:
            hid = hz[j, h, 0].reshape(512, HALF)
            oacc[...] += nn(hid, wd[j, h])
            gdl[:, cols] = nn(pr[32:48], hid)
            bk[32:48] += nt(dlt[:, cols], hid)
        elif s == 9:
            zg = hz[j, h, 1].reshape(512, HALF)
            zu = hz[j, h, 2].reshape(512, HALF)
            xacc[...] += nt(zg, wg[j, h]) + nt(zu, wu[j, h])
            ggr[:, cols] = nn(pr[0:16], zg)
            gur[:, cols] = nn(pr[16:32], zu)
            bk[0:16] += nt(gr[:, cols], zg)
            bk[16:32] += nt(ur[:, cols], zu)
        if s < 8:
            start(copies(s, j, h))

    own_pd = pd.at[x, c]
    pd_core = mcopy(own_pd, own_pd, 22, other)
    pd_right = mcopy(own_pd, own_pd, 23, at_x(xr))
    pd_left = mcopy(own_pd, own_pd, 24, at_x(xl))
    lo_pd, ro_pd, oo_pd = pd.at[xl, c], pd.at[xr, c], pd.at[xo, c]
    a_pd, b_pd = pd.at[xl, c, 0:32], pd.at[xr, c, 32:64]
    pd_pass = [
        mcopy(a_pd, a_pd, 25, at_x(xr)),
        mcopy(b_pd, b_pd, 26, at_x(xl)),
        mcopy(lo_pd, lo_pd, 27, other),
        mcopy(ro_pd, ro_pd, 28, other),
    ]
    pd_last = mcopy(oo_pd, oo_pd, 29, other)

    def final_core(k):
        return [mcopy(fs.at[1 - c, k], fr.at[k], 9 + k, other)]

    def final_half(k):
        return [
            mcopy(fs.at[c, k, xo, 0:32], th.at[0, k], 17 + k, at_x(xr)),
            mcopy(fs.at[c, k, xo, 32:64], th.at[1, k], 19 + k, at_x(xl)),
        ]

    def final_full(k):
        return [
            mcopy(fs.at[c, k, xr], tf.at[0, k], 12 + k, at_x(xr)),
            mcopy(fs.at[c, k, xl], tf.at[1, k], 14 + k, at_x(xl)),
        ]

    def reach_core(k, acc):
        for b in range(8):
            fs[b % 2, k, b // 2] = acc[b * 64 : b * 64 + 64].astype(BF16)
        start(final_core(k))

    def reach_half(k):
        wait(final_core(k))
        add_into(fs.at[c, k], fr.at[k])
        start(final_half(k))

    def reach_full(k):
        wait(final_half(k))
        add_into(fs.at[c, k, xr, 0:32], th.at[0, k])
        add_into(fs.at[c, k, xl, 32:64], th.at[1, k])
        start(final_full(k))

    def final_sum(k):
        wait(final_full(k))
        return fs[c, k, x].astype(F32) + tf[0, k].astype(F32) + tf[1, k].astype(F32)

    @pl.loop(0, GROUPS + STAGES - 1)
    def _(t):
        for s in range(STAGES + 1):
            j = t - s if s < STAGES else t - s + 1
            if s == 4:

                @pl.when(t == 4)
                def _():
                    spread_wait(nbz, 2)
                    n = jnp.sqrt(sum(nbz[k].astype(F32) for k in range(4)) + EPS)
                    nrm[...] = n
                    for k, mag in enumerate((gmag, umag)):
                        for g in range(GROUPS):
                            scl[k * 8 + g : k * 8 + g + 1] = mag[g * 512 : g * 512 + 512].reshape(1, 512)
                    scl[...] = scl[...] / n

            if s == STAGES - 1:

                @pl.when(t == STAGES - 1)
                def _():
                    wait([pd_core, pd_last])
                    pr[...] = jnp.transpose(pd[...].reshape(512, 128).astype(F32))[0:48].astype(BF16)

            if s == STAGES:

                @pl.when(t == GROUPS + STAGES - 2)
                def _():
                    reach_core(0, oacc)

            @pl.when(jnp.logical_and(j >= 0, j < GROUPS))
            def _():
                @pl.loop(0, 2)
                def _(h):
                    stage(s, j, h)

        @pl.when(t == 0)
        def _():
            lpad[...] = jnp.zeros_like(lpad)
            dpad[...] = jnp.zeros_like(dpad)
            lpad[0:16] = glt[...]
            lpad[16:32] = ult[...]
            dpad[32:48] = dr[...]
            own_z = (cot[...].astype(F32) * scd[1:2]).astype(BF16)
            pry[y] = (nt(tok[...], lpad[...]) + nt(own_z, dpad[...])).astype(BF16)
            ring_own(pry, y, at_y, 3)

        @pl.when(t < 2)
        def _():
            @pl.loop(2 * t + 1, 4 * t + 3)
            def _(g):
                merge_gu(g)

        @pl.when(t == 1)
        def _():
            nby[y] = nf[...].astype(BF16)
            ring_own(nby, y, at_y, 14)
            ring_pass(pry, y, at_y, 3)

        @pl.when(t == 2)
        def _():
            ring_pass(nby, y, at_y, 14)
            ring_wait(pry, 3)
            prz[z] = sum(pry[k].astype(F32) for k in range(4)).astype(BF16)
            ring_own(prz, z, at_z, 5)

        @pl.when(t == 3)
        def _():
            oacc[...] = jnp.zeros_like(oacc)
            xacc[...] = jnp.zeros_like(xacc)
            bk[...] = jnp.zeros_like(bk)
            ring_pass(prz, z, at_z, 5)
            ring_wait(nby, 14)
            nbz[z] = sum(nby[k].astype(F32) for k in range(4)).astype(BF16)
            spread(nbz, z, at_z, 2)

        @pl.when(t == 4)
        def _():
            ring_wait(prz, 5)
            pd[x, c] = sum(prz[k].astype(F32) for k in range(4)).astype(BF16)
            pd_core.start()
            pd_right.start()
            pd_left.start()

        @pl.when(t == 5)
        def _():
            wait([pd_right, pd_left])
            start(pd_pass)

        @pl.when(t == 6)
        def _():
            wait(pd_pass)
            pd_last.start()

        @pl.when(t == GROUPS + 3)
        def _():
            mgy[y] = mf[...].astype(BF16)
            ring_own(mgy, y, at_y, 7)

        @pl.when(t == GROUPS + 4)
        def _():
            ring_pass(mgy, y, at_y, 7)

        @pl.when(t == GROUPS + 5)
        def _():
            ring_wait(mgy, 7)
            mgz[z] = sum(mgy[k].astype(F32) for k in range(4)).astype(BF16)
            ring_own(mgz, z, at_z, 9)

        @pl.when(t == GROUPS + 6)
        def _():
            ring_pass(mgz, z, at_z, 9)

    smd[dp] = bk[:, pl.ds(pl.multiple_of(y * 128, 128), 128)].astype(BF16)
    for d in range(1, 8):
        rcopy(smd.at[dp], smd.at[dp], spread_s.at[11], spread_r.at[11], ((dp + d) % 8, mp)).start()
    reach_core(1, xacc)
    md_core = mcopy(mdc.at[c], mdc.at[c], 11, other)
    reach_half(0)
    mdc[c] = jnp.sum(oacc[...] * gath[1].reshape(512, 512).astype(F32), axis=0, keepdims=True)
    md_core.start()
    reach_half(1)
    landed(smd.at[0:7], spread_s.at[11])
    landed(smd.at[0:7], spread_r.at[11])
    smy[y] = sum(smd[k].astype(F32) for k in range(8)).astype(BF16)
    spread(smy, y, at_y, 12)
    reach_full(0)
    md_core.wait()
    mdx[x] = mdc[0] + mdc[1]
    spread(mdx, x, at_x, 13)
    reach_full(1)

    ring_wait(mgz, 9)
    mags = sum(mgz[k].astype(F32) for k in range(4)) / nrm[...]
    for g in range(GROUPS):
        ggm[:, g * 512 : g * 512 + 512] = mags[g : g + 1]
        gum[:, g * 512 : g * 512 + 512] = mags[8 + g : 9 + g]
    spread_wait(smy, 12)
    for k in range(4):
        back[:, k * 128 : k * 128 + 128] = smy[k]
    lg = nn(back[0:32], tokens())
    ggl[...] = lg[0:16]
    gul[...] = lg[16:32]
    gdr[...] = nn(back[32:48], zt[...])
    spread_wait(mdx, 13)
    gdm[...] = (mdx[0] + mdx[1] + mdx[2] + mdx[3]) / scd[0:1]
    out[...] = (final_sum(0) * scd[1:2]).astype(BF16)
    dx[...] = final_sum(1).astype(BF16)


def per_device(tok, fg, fu, fd, gl, gr, ul, ur, dl, dr, gmag, umag, dmag, cot):
    vm = pl.BlockSpec(memory_space=pltpu.VMEM)
    hbm = pl.BlockSpec(memory_space=pl.ANY)
    f = jax.ShapeDtypeStruct
    V = pltpu.VMEM
    G, C = GROUPS, HALF
    call = pl.pallas_call(
        kernel,
        out_shape=(
            f((64, 512), BF16), f((64, 512), BF16),
            f((1, 3584), F32), f((1, 3584), F32), f((1, 512), F32),
            f((16, 3584), F32), f((16, 512), F32), f((16, 3584), F32), f((16, 512), F32),
            f((16, 512), F32), f((16, 3584), F32),
        ),
        in_specs=[vm, vm, hbm, hbm, hbm] + [vm] * 9,
        out_specs=(vm,) * 11,
        scratch_shapes=[
            V((G, 2, 512, C), BF16), V((G, 2, 512, C), BF16), V((G, 2, C, 512), BF16),
            V((2, 4, 2, 64, 512), BF16), V((512, 512), BF16),
            V((2, 1, 512), F32), V((4, 1, 512), F32), V((2, 512), F32),
            V((16, 512), F32), V((4, 16, 512), BF16), V((4, 16, 512), BF16), V((16, 512), F32), V((16, 512), F32),
            V((128, 512), BF16), V((128, 512), BF16),
            V((4, 64, 128), BF16), V((4, 64, 128), BF16), V((4, 2, 64, 128), BF16), V((48, 512), BF16),
            V((G, 2, 3, 4, 4, 32, C), BF16),
            V((G, 2, 2, 3, 2, 32, C), BF16), V((G, 2, 2, 3, 4, 32, C), BF16),
            V((G, 2, 3, 4, 32, C), BF16),
            V((G, 2, 2, 3, 16, C), BF16), V((G, 2, 2, 3, 32, C), BF16),
            V((G, 2, 3, 4, 4, 32, C), BF16),
            V((16, 512), F32), V((4, 16, 512), BF16), V((4, 16, 512), BF16),
            V((512, 512), F32), V((512, 512), F32), V((48, 512), F32),
            V((2, 2, 4, 64, 512), BF16), V((2, 4, 64, 512), BF16),
            V((2, 2, 32, 512), BF16), V((2, 2, 64, 512), BF16),
            V((8, 48, 128), BF16), V((4, 48, 128), BF16), V((48, 512), BF16),
            V((2, 1, 512), F32), V((4, 1, 512), F32),
            pltpu.SemaphoreType.DMA((3, G)),
            pltpu.SemaphoreType.DMA((8, 2, 2)),
            pltpu.SemaphoreType.DMA((8, 3, 2)),
            pltpu.SemaphoreType.DMA((30,)),
            pltpu.SemaphoreType.DMA((30,)),
            pltpu.SemaphoreType.DMA((16,)),
            pltpu.SemaphoreType.DMA((16,)),
        ],
        compiler_params=pltpu.CompilerParams(
            collective_id=0, has_side_effects=True, vmem_limit_bytes=63 * 1024 * 1024
        ),
    )
    res = call(tok, cot, fg, fu, fd, gl.T, gr, ul.T, ur, dl.T, dr, gmag, umag, dmag)
    flat = (2, 3, 4)

    def finish(*refs):
        for k in range(11):
            value = refs[k][...]
            refs[k + 11][...] = value.reshape(-1) if k in flat else value

    o, d, ggm, gum, gdm, ggr, ggl, gur, gul, gdr, gdl = pl.pallas_call(
        finish,
        out_shape=tuple(
            f((r.size,) if k in flat else r.shape, r.dtype) for k, r in enumerate(res)
        ),
        in_specs=[vm] * 11,
        out_specs=(vm,) * 11,
    )(*res)
    return o, d, ggm, gum, gdm, ggr, ggl.T, gur, gul.T, gdr, gdl.T


def solution(mesh):
    in_specs = (
        P("dp", "mp"), P("mp", "dp"), P("mp", "dp"), P("dp", "mp"),
        P("mp", None), P(None, "dp"), P("mp", None), P(None, "dp"),
        P("dp", None), P(None, "mp"), P("dp"), P("dp"), P("mp"), P("dp", "mp"),
    )
    out_specs = (
        P("dp", "mp"), P("dp", "mp"), P("dp"), P("dp"), P("mp"),
        P(None, "dp"), P("mp", None), P(None, "dp"), P("mp", None), P(None, "mp"), P("dp", None),
    )
    return jax.shard_map(
        per_device, mesh=mesh, in_specs=in_specs, out_specs=out_specs, check_vma=False
    )
```

time: 156 us -> 152 us (0.974)
  Pallas kernels: 154 us -> 152 us
    pallas_call x1, Pallas kernels: 152 us -> 149 us  [per_device(): call(tok, cot, fg, fu, fd, gl.T, gr, ul.T, ur, dl.T, dr, gmag, umag, dmag)]
where the time goes in v4:
time: 152 us
  Pallas kernels  152 us (100%)
    pallas_call x1, Pallas kernels, per_device(): call(tok, cot, fg, fu, fd, gl.T, gr, ul.T, ur, dl.T, dr, gmag, umag, dmag)  149 us

profile of v4, /device:TPU:1, one launch (start us, length us, event | category | flops | bytes accessed | tf_op | source)
XLA Modules:
  0.0 152.3 jit_solution(9767876207194000733)
XLA Ops:
  0.6 149.4 %shard_map.221 = (bf16[64,512]{1,0:T(8,128)(2,1)}, bf16[64,512]{1,0:T(8,128)(2,1)}, f32[1,3584]{1,0:T(1,128)}, f32[1,3584]{1,0:T(1,128)}, f32[1,512]{1,0:T(1,128...) custom-call(bf16[64,512]{1,0:T(8,128)(2,1)} %tok.1, ...), custom_call_target="tpu_custom_call" | custom-call | tf_op jit(solution)/shard_map/pallas_call | solution.py:568
  150.1 2.3 %shard_map.222 = (bf16[64,512]{1,0:T(8,128)(2,1)}, bf16[64,512]{1,0:T(8,128)(2,1)}, f32[3584]{0:T(1024)}, f32[3584]{0:T(1024)}, f32[512]{0:T(512)}, /*index=5*/f...) custom-call(bf16[64,512]{1,0:T(8,128)(2,1)} %get-tuple-element.33.re, ...), custom_call_target="tpu_custom_call" | custom-call | tf_op jit(solution)/shard_map/pallas_call | solution.py:576

commit v5 on v4

--- a/solution.py
+++ b/solution.py
@@ -188,6 +188,7 @@
     sqd_x[x] = sqd_c[0] + sqd_c[1]
     spread(sqd_x, x, at_x, 0)
     merge_gu(0)
+    merge_gu(1)
 
     spread_wait(sqd_x, 0)
     sqd = sqd_x[0] + sqd_x[1] + sqd_x[2] + sqd_x[3]
@@ -250,8 +251,8 @@
         else:
             dr_, dl_ = at_b(br), at_b(bl)
         return [
-            rcopy(*a, ssem.at[s, j % 2, h], rsem.at[s, j % 3, h], dr_),
-            rcopy(*b, ssem.at[s, j % 2, h], rsem.at[s, j % 3, h], dl_),
+            rcopy(*a, ssem.at[s, j % 2, h], rsem.at[s, j % 4, h], dr_),
+            rcopy(*b, ssem.at[s, j % 2, h], rsem.at[s, j % 4, h], dl_),
         ]
 
     def arrived(s, j, h):
@@ -260,7 +261,7 @@
             hz.at[j, h, :, 0, 0:2], hz.at[j, h, :, 0, 0], hz.at[j, h, :, 0:2], hz.at[j, h, :, 0],
         )[s]
         landed(both, ssem.at[s, j % 2, h])
-        landed(both, rsem.at[s, j % 3, h])
+        landed(both, rsem.at[s, j % 4, h])
 
     def add_into(ref, extra):
         ref[...] = (ref[...].astype(F32) + extra[...].astype(F32)).astype(BF16)
@@ -370,10 +371,14 @@
         wait(final_full(k))
         return fs[c, k, x].astype(F32) + tf[0, k].astype(F32) + tf[1, k].astype(F32)
 
+    @pl.loop(0, 2)
+    def _(h):
+        stage(0, 0, h)
+
     @pl.loop(0, GROUPS + STAGES - 1)
     def _(t):
         for s in range(STAGES + 1):
-            j = t - s if s < STAGES else t - s + 1
+            j = t + 1 if s == 0 else t - s if s < STAGES else t - s + 1
             if s == 4:
 
                 @pl.when(t == 4)
@@ -418,7 +423,7 @@
 
         @pl.when(t < 2)
         def _():
-            @pl.loop(2 * t + 1, 4 * t + 3)
+            @pl.loop(2 * t + 2, 3 * t + 4)
             def _(g):
                 merge_gu(g)
 
@@ -555,7 +560,7 @@
             V((2, 1, 512), F32), V((4, 1, 512), F32),
             pltpu.SemaphoreType.DMA((3, G)),
             pltpu.SemaphoreType.DMA((8, 2, 2)),
-            pltpu.SemaphoreType.DMA((8, 3, 2)),
+            pltpu.SemaphoreType.DMA((8, 4, 2)),
             pltpu.SemaphoreType.DMA((30,)),
             pltpu.SemaphoreType.DMA((30,)),
             pltpu.SemaphoreType.DMA((16,)),

time: 152 us -> 152 us (level)
  no operation moved by 1% of the time
where the time goes in v5:
time: 152 us; the launch traced here: 151 us
  Pallas kernels  151 us (99%)
    pallas_call x1, Pallas kernels, per_device(): call(tok, cot, fg, fu, fd, gl.T, gr, ul.T, ur, dl.T, dr, gmag, umag, dmag)  149 us

profile of v5, /device:TPU:1, one launch (start us, length us, event | category | flops | bytes accessed | tf_op | source)
XLA Modules:
  0.0 151.5 jit_solution(1645219838515632042)
XLA Ops:
  0.6 148.6 %shard_map.221 = (bf16[64,512]{1,0:T(8,128)(2,1)}, bf16[64,512]{1,0:T(8,128)(2,1)}, f32[1,3584]{1,0:T(1,128)}, f32[1,3584]{1,0:T(1,128)}, f32[1,512]{1,0:T(1,128...) custom-call(bf16[64,512]{1,0:T(8,128)(2,1)} %tok.1, ...), custom_call_target="tpu_custom_call" | custom-call | tf_op jit(solution)/shard_map/pallas_call | solution.py:573
  149.2 2.3 %shard_map.222 = (bf16[64,512]{1,0:T(8,128)(2,1)}, bf16[64,512]{1,0:T(8,128)(2,1)}, f32[3584]{0:T(1024)}, f32[3584]{0:T(1024)}, f32[512]{0:T(512)}, /*index=5*/f...) custom-call(bf16[64,512]{1,0:T(8,128)(2,1)} %get-tuple-element.33.re, ...), custom_call_target="tpu_custom_call" | custom-call | tf_op jit(solution)/shard_map/pallas_call | solution.py:581
